TPU v7x, 32 devices: a whole 2x2x4 slice. The times are simulated.
32 devices in a mesh: gx: 8 (over z, x), gy: 2 (over core), gz: 2 (over y).
Axes of the slice: x: 2, y: 2, z: 4, core: 2. Of those that a mesh axis runs over, the one named last changes fastest.
Arguments:
- populations: float32 [19, 32, 32, 512], P(None, 'gx', 'gz', 'gy'), may hold values from 0.01 to 0.21
- nozzle_mask: int32 [32, 512], P('gx', 'gy'), may hold values 0 or 1
- wall_type: int32 [32, 512], P('gx', 'gy'), may hold values from 0 to 1
- solid_temp: float32 [32, 64, 512], P('gx', None, ('gy', 'gz')), may hold values from -6 to 6
- diffusion: float32 [32, 64, 512], P('gx', None, ('gy', 'gz')), may hold values from 0.3 to 3
- heat_load: float32 [32, 512], P('gx', ('gy', 'gz')), may hold values from 0.2 to 2
- coolant_temp: float32 [32, 512], P('gx', ('gy', 'gz')), may hold values from -2 to 0
Outputs:
- populations_next: float32 [19, 32, 32, 512], P(None, 'gx', 'gz', 'gy')
- solid_next: float32 [32, 64, 512], P('gx', None, ('gy', 'gz'))
Inputs may be any that keep to these rules, and one draw needn't show every extreme that they name: `nozzle_mask`: 1 marks a nozzle opening; it takes precedence over wall_type. `wall_type`: 1 marks an outlet cell of the plate, 0 a closed plate cell.
All inputs are finite; a program needn't handle non-finite values. No bound on the sum of `nozzle_mask` on one device may be relied on, other than what follows from the above.
Results may differ from a plain program's by a relative error of at most 0.0001.
Values sent between devices are 32-bit elements; how exact they have to be, the bound alone decides.
A program may use at most 64 MiB of HBM per device.

v0:
```python
import jax
import jax.numpy as jnp
import numpy as np
from jax import lax
from jax.sharding import PartitionSpec as P

JET_SPEED = 0.1
H_BASE = 0.5
H_GAIN = 40.0
SHEAR_RATE = 1.6
ODD_RATE = 1.2
EVEN_RATE = 1.4


def broadcast(block, axis, holder):
    block = jnp.where(lax.axis_index(axis) == holder, block, jnp.zeros_like(block))
    return lax.psum(block, axis)


def passed_along(value, axis, steps):
    count = lax.axis_size(axis)
    pairs = [(source, (source + steps) % count) for source in range(count)]
    return lax.ppermute(value, axis, pairs)


def from_behind(block, axis, distance):
    devices = range(lax.axis_size(axis))
    route = [(i - distance, i) for i in devices if i - distance in devices]
    return lax.ppermute(block, axis, route)


def padded(block, sides, width):
    for axis, dim in sides:
        count = lax.axis_size(axis)
        forward = [(i, i + 1) for i in range(count - 1)]
        forward.append((count - 1, 0))
        backward = [(target, source) for source, target in forward]
        low = lax.ppermute(
            lax.slice_in_dim(block, block.shape[dim] - width, None, axis=dim), axis, forward
        )
        high = lax.ppermute(lax.slice_in_dim(block, 0, width, axis=dim), axis, backward)
        block = jnp.concatenate([low, block, high], axis=dim)
    return block


def velocity_table():
    return np.array(
        [
            [0, 0, 0],
            [1, 0, 0],
            [-1, 0, 0],
            [0, 1, 0],
            [0, -1, 0],
            [0, 0, 1],
            [0, 0, -1],
            [1, 1, 0],
            [-1, -1, 0],
            [1, -1, 0],
            [-1, 1, 0],
            [1, 0, 1],
            [-1, 0, -1],
            [1, 0, -1],
            [-1, 0, 1],
            [0, 1, 1],
            [0, -1, -1],
            [0, 1, -1],
            [0, -1, 1],
        ],
        dtype=np.int32,
    )


def weight_table():
    return np.array([1.0 / 3.0] + [1.0 / 18.0] * 6 + [1.0 / 36.0] * 12, dtype=np.float32)


def opposite_of(member):
    table = velocity_table()
    for other in range(table.shape[0]):
        if np.all(table[other] == -table[member]):
            return other
    return member


def relax_table():
    table = velocity_table().astype(np.float32)
    comp_a = table[:, 0]
    comp_b = table[:, 1]
    comp_c = table[:, 2]
    monomials = [
        comp_a * 0.0 + 1.0,
        comp_a,
        comp_b,
        comp_c,
        comp_a * comp_a,
        comp_b * comp_b,
        comp_c * comp_c,
        comp_a * comp_b,
        comp_b * comp_c,
        comp_a * comp_c,
        comp_a * comp_c * comp_c,
        comp_a * comp_b * comp_b,
        comp_c * comp_a * comp_a,
        comp_c * comp_b * comp_b,
        comp_b * comp_a * comp_a,
        comp_b * comp_c * comp_c,
        comp_a * comp_a * comp_c * comp_c,
        comp_a * comp_a * comp_b * comp_b,
        comp_c * comp_c * comp_b * comp_b,
    ]
    rates = np.array(
        [0.0] * 4 + [SHEAR_RATE] * 6 + [ODD_RATE] * 6 + [EVEN_RATE] * 3, dtype=np.float32
    )
    ortho = []
    for monomial in monomials:
        vector = monomial.copy()
        for earlier in ortho:
            vector = vector - np.dot(earlier, vector) * earlier
        ortho.append(vector / np.sqrt(np.dot(vector, vector)))
    gram = np.stack(ortho)
    return (gram.T @ (rates[:, None] * gram)).astype(np.float32)


def collide(pops):
    table = jnp.asarray(velocity_table().astype(np.float32))
    weights = jnp.asarray(weight_table())
    density = jnp.sum(pops, axis=0)
    momentum = jnp.einsum("qc,qxzy->cxzy", table, pops, precision=lax.Precision.HIGHEST)
    velocity = momentum / density[None]
    project = jnp.einsum("qc,cxzy->qxzy", table, velocity, precision=lax.Precision.HIGHEST)
    square = jnp.sum(velocity * velocity, axis=0)
    equil = (
        weights[:, None, None, None]
        * density[None]
        * (1.0 + 3.0 * project + 4.5 * project * project - 1.5 * square[None])
    )
    relaxed = jnp.einsum(
        "pq,qxzy->pxzy", jnp.asarray(relax_table()), pops - equil, precision=lax.Precision.HIGHEST
    )
    return (pops - relaxed, density, velocity)


def wall_coefficient(velocity_plane):
    return H_BASE + H_GAIN * jnp.sum(velocity_plane * velocity_plane, axis=0)


def apply_walls(moved, post, nozzle, outlet_kind, at_bottom, at_top):
    table = velocity_table()
    weights = weight_table()
    layers = []
    for member in range(table.shape[0]):
        layer = moved[member]
        other = opposite_of(member)
        if table[member, 2] > 0:
            bottom_value = post[other][:, 0, :]
            layer = layer.at[:, 0, :].set(jnp.where(at_bottom, bottom_value, layer[:, 0, :]))
        if table[member, 2] < 0:
            closed_value = post[other][:, -1, :]
            inlet_value = closed_value + 6.0 * float(weights[member]) * JET_SPEED
            outlet_value = post[member][:, -1, :]
            top_value = jnp.where(
                nozzle == 1, inlet_value, jnp.where(outlet_kind == 1, outlet_value, closed_value)
            )
            layer = layer.at[:, -1, :].set(jnp.where(at_top, top_value, layer[:, -1, :]))
        layers.append(layer)
    return jnp.stack(layers)


def sweep_core(temp, cond, told, load, heat, coolant, neighbours):
    numer = told
    denom = jnp.ones_like(told)
    for near_temp, near_cond in neighbours:
        link = 0.5 * (cond + near_cond)
        numer = numer + link * near_temp
        denom = denom + link
    link = 0.5 * (cond[:, 1:] + cond[:, :-1])
    edge = jnp.zeros_like(cond[:, :1])
    numer = numer + jnp.concatenate([link * temp[:, 1:], edge], axis=1)
    denom = denom + jnp.concatenate([link, edge], axis=1)
    numer = numer + jnp.concatenate([edge, link * temp[:, :-1]], axis=1)
    denom = denom + jnp.concatenate([edge, link], axis=1)
    numer = numer.at[:, 0].add(load)
    numer = numer.at[:, -1].add(heat * coolant)
    denom = denom.at[:, -1].add(heat)
    return numer / denom


def cycle_of(temp, cond):
    return [
        (temp[:-2, :, 1:-1], cond[:-2, :, 1:-1]),
        (temp[2:, :, 1:-1], cond[2:, :, 1:-1]),
        (temp[1:-1, :, :-2], cond[1:-1, :, :-2]),
        (temp[1:-1, :, 2:], cond[1:-1, :, 2:]),
    ]


def body(populations, nozzle_mask, wall_type, solid_temp, diffusion, heat_load, coolant_temp):
    table = velocity_table()
    count = table.shape[0]
    post, density, velocity = collide(populations)
    heat_local = wall_coefficient(velocity[:, :, 0, :])
    tile_width = heat_load.shape[1]
    full_plane = broadcast(heat_local, "gz", 0)
    heat = lax.dynamic_slice_in_dim(full_plane, lax.axis_index("gz") * tile_width, tile_width, 1)
    layers = [post[member] for member in range(count)]
    rising = [member for member in range(count) if table[member, 0] > 0]
    falling = [member for member in range(count) if table[member, 0] < 0]
    up_plane = passed_along(jnp.stack([layers[member][-1:] for member in rising]), "gx", 1)
    down_plane = passed_along(jnp.stack([layers[member][:1] for member in falling]), "gx", -1)
    for position, member in enumerate(rising):
        layers[member] = jnp.concatenate([up_plane[position], layers[member][:-1]], axis=0)
    for position, member in enumerate(falling):
        layers[member] = jnp.concatenate([layers[member][1:], down_plane[position]], axis=0)
    rising = [member for member in range(count) if table[member, 1] > 0]
    falling = [member for member in range(count) if table[member, 1] < 0]
    up_plane = passed_along(jnp.stack([layers[member][:, :, -1:] for member in rising]), "gy", 1)
    down_plane = passed_along(jnp.stack([layers[member][:, :, :1] for member in falling]), "gy", -1)
    for position, member in enumerate(rising):
        layers[member] = jnp.concatenate([up_plane[position], layers[member][:, :, :-1]], axis=2)
    for position, member in enumerate(falling):
        layers[member] = jnp.concatenate([layers[member][:, :, 1:], down_plane[position]], axis=2)
    rising = [member for member in range(count) if table[member, 2] > 0]
    falling = [member for member in range(count) if table[member, 2] < 0]
    up_plane = from_behind(jnp.stack([layers[member][:, -1:] for member in rising]), "gz", 1)
    down_plane = from_behind(jnp.stack([layers[member][:, :1] for member in falling]), "gz", -1)
    for position, member in enumerate(rising):
        layers[member] = jnp.concatenate([up_plane[position], layers[member][:, :-1]], axis=1)
    for position, member in enumerate(falling):
        layers[member] = jnp.concatenate([layers[member][:, 1:], down_plane[position]], axis=1)
    moved = jnp.stack(layers)
    at_bottom = lax.axis_index("gz") == 0
    at_top = lax.axis_index("gz") == lax.axis_size("gz") - 1
    populations_next = apply_walls(moved, post, nozzle_mask, wall_type, at_bottom, at_top)
    temp_ext, cond_ext = (
        padded(solid_temp, (("gx", 0), (("gy", "gz"), 2)), 1),
        padded(diffusion, (("gx", 0), (("gy", "gz"), 2)), 1),
    )
    first = sweep_core(
        solid_temp,
        diffusion,
        solid_temp,
        heat_load,
        heat,
        coolant_temp,
        cycle_of(temp_ext, cond_ext),
    )
    first_ext = padded(first, (("gx", 0), (("gy", "gz"), 2)), 1)
    solid_next = sweep_core(
        first, diffusion, solid_temp, heat_load, heat, coolant_temp, cycle_of(first_ext, cond_ext)
    )
    return (populations_next, solid_next)


def solution(mesh):
    placed = (
        P(None, "gx", "gz", "gy"),
        P("gx", "gy"),
        P("gx", "gy"),
        P("gx", None, ("gy", "gz")),
        P("gx", None, ("gy", "gz")),
        P("gx", ("gy", "gz")),
        P("gx", ("gy", "gz")),
    )
    return jax.shard_map(
        body,
        mesh=mesh,
        in_specs=placed,
        out_specs=(P(None, "gx", "gz", "gy"), P("gx", None, ("gy", "gz"))),
        check_vma=False,
    )
```

profile of v0, /device:TPU:0, one launch (start us, length us, event | category | flops | bytes accessed | tf_op | source)
XLA Modules:
  0.0 105.2 jit_solution(1134760025313323833)
XLA Ops:
  0.7 1.5 %fusion.118 = (f32[1,64,128]{2,1,0:T(8,128)}, f32[1,64,128]{2,1,0:T(8,128)}) fusion(f32[4,64,128]{2,1,0:T(8,128)} %param.46), kind=kLoop, calls=%fused_computation.303 | loop fusion | bytes 131072 | tf_op jit(solution)/shard_map/slice | solution.py:41
  2.2 2.9 %collective-permute-start.6 = (f32[1,64,128]{2,1,0:T(8,128)}, f32[1,64,128]{2,1,0:T(8,128)S(1)}, u32[]{:S(2)}, u32[]{:S(2)}) collective-permute-start(f32[1,64,128]{2,1,0:T(8,128)} %get-tuple-element.252), channel_id=1, source_target_pairs={{0,4},{4,8},{8,12},{12,16},{16,20},{20,24},{24,28},{28,0},{1,5},{5... | collective-permute-start | bytes 98312 | tf_op jit(solution)/shard_map/ppermute | solution.py:38
  5.1 3.0 %collective-permute-start.8 = (f32[1,64,128]{2,1,0:T(8,128)}, f32[1,64,128]{2,1,0:T(8,128)S(1)}, u32[]{:S(2)}, u32[]{:S(2)}) collective-permute-start(f32[1,64,128]{2,1,0:T(8,128)} %get-tuple-element.251), channel_id=1, source_target_pairs={{4,0},{8,4},{12,8},{16,12},{20,16},{24,20},{28,24},{0,28},{5,1},{9... | collective-permute-start | bytes 98312 | tf_op jit(solution)/shard_map/ppermute | solution.py:41
  8.1 1.4 %fusion.117 = (f32[1,64,128]{2,1,0:T(8,128)}, f32[1,64,128]{2,1,0:T(8,128)}) fusion(f32[4,64,128]{2,1,0:T(8,128)} %param.45), kind=kLoop, calls=%fused_computation.302 | loop fusion | bytes 131072 | tf_op jit(solution)/shard_map/slice | solution.py:41
  9.5 4.7 %collective-permute-start.9 = (f32[1,64,128]{2,1,0:T(8,128)}, f32[1,64,128]{2,1,0:T(8,128)}, u32[]{:S(2)}, u32[]{:S(2)}) collective-permute-start(f32[1,64,128]{2,1,0:T(8,128)} %get-tuple-element.249), channel_id=1, source_target_pairs={{4,0},{8,4},{12,8},{16,12},{20,16},{24,20},{28,24},{0,28},{5,1},{9... | collective-permute-start | bytes 98312 | tf_op jit(solution)/shard_map/ppermute | solution.py:41
  14.3 1.4 %reduce_sum.27 = f32[4,16,256]{2,1,0:T(8,128)S(1)} reduce(f32[19,4,16,256]{3,2,1,0:T(8,128)} %param.42, f32[]{:T(128)} %constant.374.clone.1), dimensions={0}, to_apply=%region_0.0 | reduce | flops 294912 | bytes 1310724 | tf_op jit(solution)/shard_map/reduce_sum | solution.py:127
  15.7 1.7 %multiply_reduce_fusion = (f32[4,16,256]{2,1,0:T(8,128)S(1)}, f32[3,4,16,256]{3,0,2,1:T(4,128)S(1)}) fusion(f32[4,16,256]{2,1,0:T(8,128)S(1)} %reduce_sum.27, f32[19,3,1,1]{0,1,3,2:T(4,128)S(1)} %copy-done.30, f32[19,4,16,256]{3,2,1,0:T(8,128)S(1)} %copy-done), kind=kOutput, calls=%fused_computation.19 | convolution fusion | flops 11337728 | bytes 1573092 | tf_op jit(solution)/shard_map/qc,qxzy->cxzy/dot_general | solution.py:128
  17.4 1.5 %fusion.119 = f32[19,4,16,256]{3,0,2,1:T(8,128)S(1)} fusion(f32[19,3,1,1]{0,1,3,2:T(4,128)S(1)} %copy-done.30, f32[3,4,16,256]{3,0,2,1:T(4,128)S(1)} %get-tuple-element.292), kind=kOutput, calls=%fused_computation.304 | convolution fusion | flops 11206656 | bytes 1442020 | tf_op jit(solution)/shard_map/qc,cxzy->qxzy/dot_general | solution.py:130
  18.9 2.3 %fusion.2 = f32[19,4,16,256]{3,0,2,1:T(8,128)S(1)} fusion(f32[19,19,1,1]{1,0,3,2:T(8,128)S(1)} %copy-done.21, f32[19,4,16,256]{3,2,1,0:T(8,128)S(1)} %copy-done, f32[19,4,16,256]{3,0,2,1:T(8,128)S(1)} %fusion.119, f32[4,16,256]{2,1,0:T(8,128)S(1)} %broadcast_multiply_fusion, f32[4,16,256]{2,1,0:T(8,128)S(1)} %reduce_sum.27, f32[19]{0:T(128)S(1)} %copy-done.32), kind=kOutput, calls=%fused_computation.4 | convolution fusion | flops 73777152 | bytes 3868144 | tf_op jit(solution)/shard_map/pq,qxzy->pxzy/dot_general | solution.py:137
  22.5 0.8 stack.155
  23.3 0.7 fusion.111
  24.0 0.7 fusion.110
  24.8 4.9 %psum.7 = f32[4,256]{1,0:T(4,128)S(1)} all-reduce(f32[4,256]{1,0:T(4,128)S(1)} %add_select_fusion), channel_id=1, replica_groups=mesh['gx'=8,'gy'=2,'gz'=2] {'gz'}, use_global_device_ids=true, to_apply=%region_3.4 | all-reduce | flops 1024 | bytes 8192 | tf_op jit(solution)/shard_map/psum | solution.py:17
  31.6 0.7 copy_bitcast_fusion.4
  32.9 0.7 copy_bitcast_fusion
  34.4 0.8 stack.153
  35.2 2.0 %collective-permute-start = (f32[5,1,16,256]{3,0,2,1:T(8,128)}, f32[5,1,16,256]{3,0,2,1:T(8,128)}, u32[]{:S(2)}, u32[]{:S(2)}) collective-permute-start(f32[5,1,16,256]{3,0,2,1:T(8,128)} %stack.153), channel_id=1, source_target_pairs={{0,4},{4,8},{8,12},{12,16},{16,20},{20,24},{24,28},{28,0},{1,5},{5... | collective-permute-start | bytes 245768 | tf_op jit(solution)/shard_map/ppermute | solution.py:23
  37.4 1.8 %collective-permute-start.10 = (f32[6,64,1]{2,1,0:T(8,128)S(1)}, f32[6,64,1]{2,1,0:T(8,128)S(1)}, u32[]{:S(2)}, u32[]{:S(2)}) collective-permute-start(f32[6,64,1]{2,1,0:T(8,128)S(1)} %get-tuple-element.246), channel_id=1, source_target_pairs={{0,1},{1,2},{2,3},{3,0},{4,5},{5,6},{6,7},{7,4},{8,9},{9,10},{10,1... | collective-permute-start | bytes 4616 | tf_op jit(solution)/shard_map/ppermute | solution.py:38
  39.2 0.8 constant_dynamic-update-slice_fusion.44
  40.0 0.8 constant_dynamic-update-slice_fusion.42
  40.8 2.0 %collective-permute-start.11 = (f32[6,64,1]{2,1,0:T(8,128)S(1)}, f32[6,64,1]{2,1,0:T(8,128)S(1)}, u32[]{:S(2)}, u32[]{:S(2)}) collective-permute-start(f32[6,64,1]{2,1,0:T(8,128)S(1)} %get-tuple-element.243), channel_id=1, source_target_pairs={{0,1},{1,2},{2,3},{3,0},{4,5},{5,6},{6,7},{7,4},{8,9},{9,10},{10,1... | collective-permute-start | bytes 4616 | tf_op jit(solution)/shard_map/ppermute | solution.py:38
  42.9 1.5 %collective-permute-done.10 = f32[6,64,1]{2,1,0:T(8,128)S(1)} collective-permute-done((f32[6,64,1]{2,1,0:T(8,128)S(1)}, f32[6,64,1]{2,1,0:T(8,128)S(1)}, u32[]{:S(2)}, u32[]{:S(2)}) %collective-permute-start.10) | collective-permute-done | bytes 1568 | tf_op jit(solution)/shard_map/ppermute | solution.py:38
  44.3 4.7 %collective-permute-done.12 = f32[6,64,1]{2,1,0:T(8,128)S(1)} collective-permute-done((f32[6,64,1]{2,1,0:T(8,128)S(1)}, f32[6,64,1]{2,1,0:T(8,128)S(1)}, u32[]{:S(2)}, u32[]{:S(2)}) %collective-permute-start.12) | collective-permute-done | bytes 1568 | tf_op jit(solution)/shard_map/ppermute | solution.py:41
  49.3 3.5 %collective-permute-done.11 = f32[6,64,1]{2,1,0:T(8,128)S(1)} collective-permute-done((f32[6,64,1]{2,1,0:T(8,128)S(1)}, f32[6,64,1]{2,1,0:T(8,128)S(1)}, u32[]{:S(2)}, u32[]{:S(2)}) %collective-permute-start.11) | collective-permute-done | bytes 1568 | tf_op jit(solution)/shard_map/ppermute | solution.py:38
  52.8 4.5 %collective-permute-done.13 = f32[6,64,1]{2,1,0:T(8,128)S(1)} collective-permute-done((f32[6,64,1]{2,1,0:T(8,128)S(1)}, f32[6,64,1]{2,1,0:T(8,128)S(1)}, u32[]{:S(2)}, u32[]{:S(2)}) %collective-permute-start.13) | collective-permute-done | bytes 1568 | tf_op jit(solution)/shard_map/ppermute | solution.py:41
  57.2 0.9 fusion.32
  58.6 4.7 %collective-permute-start.15 = (f32[1,64,128]{2,1,0:T(8,128)S(1)}, f32[1,64,128]{2,1,0:T(8,128)}, u32[]{:S(2)}, u32[]{:S(2)}) collective-permute-start(f32[1,64,128]{2,1,0:T(8,128)S(1)} %get-tuple-element.248), channel_id=1, source_target_pairs={{4,0},{8,4},{12,8},{16,12},{20,16},{24,20},{28,24},{0,28},{5,1},{9... | collective-permute-start | bytes 98312 | tf_op jit(solution)/shard_map/ppermute | solution.py:41
  63.3 0.7 slice_reduce_fusion
  64.9 0.7 slice.1057
  65.8 0.8 copy.287
  69.0 0.9 copy.288
  69.8 0.8 slice.1112
  71.9 0.8 pad_maximum_fusion
  72.9 1.7 %collective-permute-start.17 = (f32[6,64,1]{2,1,0:T(8,128)S(1)}, f32[6,64,1]{2,1,0:T(8,128)S(1)}, u32[]{:S(2)}, u32[]{:S(2)}) collective-permute-start(f32[6,64,1]{2,1,0:T(8,128)S(1)} %get-tuple-element.242), channel_id=1, source_target_pairs={{1,0},{2,1},{3,2},{0,3},{5,4},{6,5},{7,6},{4,7},{9,8},{10,9},{11,1... | collective-permute-start | bytes 4616 | tf_op jit(solution)/shard_map/ppermute | solution.py:41
  74.6 5.4 %collective-permute-done.16 = f32[6,64,1]{2,1,0:T(8,128)S(1)} collective-permute-done((f32[6,64,1]{2,1,0:T(8,128)S(1)}, f32[6,64,1]{2,1,0:T(8,128)S(1)}, u32[]{:S(2)}, u32[]{:S(2)}) %collective-permute-start.16) | collective-permute-done | bytes 1568 | tf_op jit(solution)/shard_map/ppermute | solution.py:38
  80.0 3.3 %collective-permute-done.17 = f32[6,64,1]{2,1,0:T(8,128)S(1)} collective-permute-done((f32[6,64,1]{2,1,0:T(8,128)S(1)}, f32[6,64,1]{2,1,0:T(8,128)S(1)}, u32[]{:S(2)}, u32[]{:S(2)}) %collective-permute-start.17) | collective-permute-done | bytes 1568 | tf_op jit(solution)/shard_map/ppermute | solution.py:41
  83.3 1.0 fusion.22
  85.3 1.3 %slice_bitcast_fusion.3 = (f32[1,16,256]{2,0,1:T(1,128)S(1)}, f32[1,16,256]{2,0,1:T(1,128)S(1)}, f32[1,16,256]{2,0,1:T(1,128)S(1)}, f32[1,16,256]{2,0,1:T(1,128)S(1)}, f32[1,16,256]{2,0,1:T(1,128)S(1)}) fusion(f32[5,1,16,256]{3,0,2,1:T(8,128)} %collective-permute-done.1), kind=kLoop, calls=%fused_computation.197 | loop fusion | bytes 163840 | tf_op jit(solution)/shard_map/squeeze | solution.py:213
  86.9 1.3 %slice_bitcast_fusion.2 = (f32[1,16,256]{2,0,1:T(1,128)S(1)}, f32[1,16,256]{2,0,1:T(1,128)S(1)}, f32[1,16,256]{2,0,1:T(1,128)S(1)}, f32[1,16,256]{2,0,1:T(1,128)S(1)}, f32[1,16,256]{2,0,1:T(1,128)S(1)}) fusion(f32[5,1,16,256]{3,0,2,1:T(8,128)} %collective-permute-done), kind=kLoop, calls=%fused_computation.196 | loop fusion | bytes 163840 | tf_op jit(solution)/shard_map/squeeze | solution.py:211
  90.6 1.3 %collective-permute-start.5 = (f32[5,4,1,256]{3,1,2,0:T(4,128)S(1)}, f32[5,4,1,256]{3,1,2,0:T(4,128)S(1)}, u32[]{:S(2)}, u32[]{:S(2)}) collective-permute-start(f32[5,4,1,256]{3,1,2,0:T(4,128)S(1)} %constant_dynamic-update-slice_fusion.15), channel_id=1, source_target_pairs={{1,0},{3,2},{5,4},{7,6},{9,8},{11,10},{13,12},{15,14},{17,16},{19,... | collective-permute-start | bytes 61448 | tf_op jit(solution)/shard_map/ppermute | solution.py:29
  93.0 3.3 %collective-permute-done.5 = f32[5,4,1,256]{3,1,2,0:T(4,128)S(1)} collective-permute-done((f32[5,4,1,256]{3,1,2,0:T(4,128)S(1)}, f32[5,4,1,256]{3,1,2,0:T(4,128)S(1)}, u32[]{:S(2)}, u32[]{:S(2)}) %collective-permute-start.5) | collective-permute-done | bytes 20512 | tf_op jit(solution)/shard_map/ppermute | solution.py:29
  96.4 0.7 fusion.94
  97.3 1.6 %collective-permute-start.4 = (f32[5,4,1,256]{3,2,1,0:T(1,128)S(1)}, f32[5,4,1,256]{3,2,1,0:T(1,128)S(1)}, u32[]{:S(2)}, u32[]{:S(2)}) collective-permute-start(f32[5,4,1,256]{3,2,1,0:T(1,128)S(1)} %copy.165), channel_id=1, source_target_pairs={{0,1},{2,3},{4,5},{6,7},{8,9},{10,11},{12,13},{14,15},{16,17},{18,... | collective-permute-start | bytes 61448 | tf_op jit(solution)/shard_map/ppermute | solution.py:29
  99.1 1.3 %collective-permute-done.4 = f32[5,4,1,256]{3,2,1,0:T(1,128)S(1)} collective-permute-done((f32[5,4,1,256]{3,2,1,0:T(1,128)S(1)}, f32[5,4,1,256]{3,2,1,0:T(1,128)S(1)}, u32[]{:S(2)}, u32[]{:S(2)}) %collective-permute-start.4) | collective-permute-done | bytes 20512 | tf_op jit(solution)/shard_map/ppermute | solution.py:29
  100.4 0.8 broadcast_select_fusion
  101.5 0.7 fusion.80
  103.1 0.7 fusion.87
  103.9 1.3 %copy.188 = f32[19,4,16,256]{3,2,1,0:T(8,128)} copy(f32[19,4,16,256]{3,1,2,0:T(4,128)S(1)} %constant_dynamic-update-slice_fusion.20) | data formatting | bytes 2490368
  (232 shorter events, 16.1 us)
Async XLA Ops:
  0.6 15.0 %copy-start.30 = (f32[19,3,1,1]{0,1,3,2:T(4,128)S(1)}, f32[19,3,1,1]{0,1,3,2:T(4,128)}, u32[]{:S(2)}) copy-start(f32[19,3,1,1]{0,1,3,2:T(4,128)} %constant.413) | copy-start | bytes 688
  0.6 15.0 %copy-start = (f32[19,4,16,256]{3,2,1,0:T(8,128)S(1)}, f32[19,4,16,256]{3,2,1,0:T(8,128)}, u32[]{:S(2)}) copy-start(f32[19,4,16,256]{3,2,1,0:T(8,128)} %param.42) | copy-start | bytes 3735556
  2.2 33.0 %collective-permute-start.6 = (f32[1,64,128]{2,1,0:T(8,128)}, f32[1,64,128]{2,1,0:T(8,128)S(1)}, u32[]{:S(2)}, u32[]{:S(2)}) collective-permute-start(f32[1,64,128]{2,1,0:T(8,128)} %get-tuple-element.252), channel_id=1, source_target_pairs={{0,4},{4,8},{8,12},{12,16},{16,20},{20,24},{24,28},{28,0},{1,5},{5... | collective-permute-start | bytes 98312 | tf_op jit(solution)/shard_map/ppermute | solution.py:38
  5.1 32.1 %collective-permute-start.8 = (f32[1,64,128]{2,1,0:T(8,128)}, f32[1,64,128]{2,1,0:T(8,128)S(1)}, u32[]{:S(2)}, u32[]{:S(2)}) collective-permute-start(f32[1,64,128]{2,1,0:T(8,128)} %get-tuple-element.251), channel_id=1, source_target_pairs={{4,0},{8,4},{12,8},{16,12},{20,16},{24,20},{28,24},{0,28},{5,1},{9... | collective-permute-start | bytes 98312 | tf_op jit(solution)/shard_map/ppermute | solution.py:41
  9.5 29.6 %collective-permute-start.7 = (f32[1,64,128]{2,1,0:T(8,128)}, f32[1,64,128]{2,1,0:T(8,128)}, u32[]{:S(2)}, u32[]{:S(2)}) collective-permute-start(f32[1,64,128]{2,1,0:T(8,128)} %get-tuple-element.250), channel_id=1, source_target_pairs={{0,4},{4,8},{8,12},{12,16},{16,20},{20,24},{24,28},{28,0},{1,5},{5... | collective-permute-start | bytes 98312 | tf_op jit(solution)/shard_map/ppermute | solution.py:38
  9.5 30.4 %collective-permute-start.9 = (f32[1,64,128]{2,1,0:T(8,128)}, f32[1,64,128]{2,1,0:T(8,128)}, u32[]{:S(2)}, u32[]{:S(2)}) collective-permute-start(f32[1,64,128]{2,1,0:T(8,128)} %get-tuple-element.249), channel_id=1, source_target_pairs={{4,0},{8,4},{12,8},{16,12},{20,16},{24,20},{28,24},{0,28},{5,1},{9... | collective-permute-start | bytes 98312 | tf_op jit(solution)/shard_map/ppermute | solution.py:41
  23.2 62.1 %collective-permute-start.1 = (f32[5,1,16,256]{3,0,2,1:T(8,128)}, f32[5,1,16,256]{3,0,2,1:T(8,128)}, u32[]{:S(2)}, u32[]{:S(2)}) collective-permute-start(f32[5,1,16,256]{3,0,2,1:T(8,128)} %stack.155), channel_id=1, source_target_pairs={{0,28},{4,0},{8,4},{12,8},{16,12},{20,16},{24,20},{28,24},{1,29},{... | collective-permute-start | bytes 245768 | tf_op jit(solution)/shard_map/ppermute | solution.py:23
  24.8 6.8 %copy-start.15 = (f32[1,3,16,256]{3,2,1,0:T(8,128)S(1)}, f32[1,3,16,256]{3,2,1,0:T(8,128)}, u32[]{:S(2)}) copy-start(f32[1,3,16,256]{3,2,1,0:T(8,128)} %get-tuple-element.220) | copy-start | bytes 147460
  24.8 6.8 %copy-start.16 = (f32[1,3,16,256]{3,2,1,0:T(8,128)S(1)}, f32[1,3,16,256]{3,2,1,0:T(8,128)}, u32[]{:S(2)}) copy-start(f32[1,3,16,256]{3,2,1,0:T(8,128)} %get-tuple-element.222) | copy-start | bytes 147460
  24.8 8.9 %copy-start.29 = (f32[4,128]{1,0:T(4,128)S(1)}, f32[4,128]{1,0:T(4,128)}, u32[]{:S(2)}) copy-start(f32[4,128]{1,0:T(4,128)} %param.48) | copy-start | bytes 6148
  24.8 9.5 %copy-start.18 = (f32[1,1,16,256]{3,2,1,0:T(8,128)S(1)}, f32[1,1,16,256]{3,2,1,0:T(8,128)}, u32[]{:S(2)}) copy-start(f32[1,1,16,256]{3,2,1,0:T(8,128)} %get-tuple-element.238) | copy-start | bytes 49156
  24.8 9.5 %copy-start.17 = (f32[1,1,16,256]{3,2,1,0:T(8,128)S(1)}, f32[1,1,16,256]{3,2,1,0:T(8,128)}, u32[]{:S(2)}) copy-start(f32[1,1,16,256]{3,2,1,0:T(8,128)} %get-tuple-element.237) | copy-start | bytes 49156
  33.7 24.6 %copy-start.19 = (f32[4,128]{1,0:T(4,128)}, f32[4,128]{1,0:T(4,128)S(1)}, u32[]{:S(2)}) copy-start(f32[4,128]{1,0:T(4,128)S(1)} %get-tuple-element.199) | copy-start | bytes 6148
  35.2 51.7 %collective-permute-start = (f32[5,1,16,256]{3,0,2,1:T(8,128)}, f32[5,1,16,256]{3,0,2,1:T(8,128)}, u32[]{:S(2)}, u32[]{:S(2)}) collective-permute-start(f32[5,1,16,256]{3,0,2,1:T(8,128)} %stack.153), channel_id=1, source_target_pairs={{0,4},{4,8},{8,12},{12,16},{16,20},{20,24},{24,28},{28,0},{1,5},{5... | collective-permute-start | bytes 245768 | tf_op jit(solution)/shard_map/ppermute | solution.py:23
  37.4 7.0 %collective-permute-start.10 = (f32[6,64,1]{2,1,0:T(8,128)S(1)}, f32[6,64,1]{2,1,0:T(8,128)S(1)}, u32[]{:S(2)}, u32[]{:S(2)}) collective-permute-start(f32[6,64,1]{2,1,0:T(8,128)S(1)} %get-tuple-element.246), channel_id=1, source_target_pairs={{0,1},{1,2},{2,3},{3,0},{4,5},{5,6},{6,7},{7,4},{8,9},{9,10},{10,1... | collective-permute-start | bytes 4616 | tf_op jit(solution)/shard_map/ppermute | solution.py:38
  39.1 10.0 %collective-permute-start.12 = (f32[6,64,1]{2,1,0:T(8,128)S(1)}, f32[6,64,1]{2,1,0:T(8,128)S(1)}, u32[]{:S(2)}, u32[]{:S(2)}) collective-permute-start(f32[6,64,1]{2,1,0:T(8,128)S(1)} %get-tuple-element.245), channel_id=1, source_target_pairs={{1,0},{2,1},{3,2},{0,3},{5,4},{6,5},{7,6},{4,7},{9,8},{10,9},{11,1... | collective-permute-start | bytes 4616 | tf_op jit(solution)/shard_map/ppermute | solution.py:41
  40.8 11.9 %collective-permute-start.11 = (f32[6,64,1]{2,1,0:T(8,128)S(1)}, f32[6,64,1]{2,1,0:T(8,128)S(1)}, u32[]{:S(2)}, u32[]{:S(2)}) collective-permute-start(f32[6,64,1]{2,1,0:T(8,128)S(1)} %get-tuple-element.243), channel_id=1, source_target_pairs={{0,1},{1,2},{2,3},{3,0},{4,5},{5,6},{6,7},{7,4},{8,9},{9,10},{10,1... | collective-permute-start | bytes 4616 | tf_op jit(solution)/shard_map/ppermute | solution.py:38
  44.3 13.9 %copy-start.22 = (f32[4,128]{1,0:T(4,128)S(1)}, f32[4,128]{1,0:T(4,128)}, u32[]{:S(2)}) copy-start(f32[4,128]{1,0:T(4,128)} %param.47) | copy-start | bytes 6148
  44.3 12.9 %collective-permute-start.13 = (f32[6,64,1]{2,1,0:T(8,128)S(1)}, f32[6,64,1]{2,1,0:T(8,128)S(1)}, u32[]{:S(2)}, u32[]{:S(2)}) collective-permute-start(f32[6,64,1]{2,1,0:T(8,128)S(1)} %get-tuple-element.244), channel_id=1, source_target_pairs={{1,0},{2,1},{3,2},{0,3},{5,4},{6,5},{7,6},{4,7},{9,8},{10,9},{11,1... | collective-permute-start | bytes 4616 | tf_op jit(solution)/shard_map/ppermute | solution.py:41
  58.2 7.5 %copy-start.14 = (f32[1,3,16,256]{3,2,1,0:T(8,128)S(1)}, f32[1,3,16,256]{3,2,1,0:T(8,128)}, u32[]{:S(2)}) copy-start(f32[1,3,16,256]{3,2,1,0:T(8,128)} %get-tuple-element.224) | copy-start | bytes 147460
  58.2 7.5 %copy-start.13 = (f32[1,3,16,256]{3,2,1,0:T(8,128)S(1)}, f32[1,3,16,256]{3,2,1,0:T(8,128)}, u32[]{:S(2)}) copy-start(f32[1,3,16,256]{3,2,1,0:T(8,128)} %get-tuple-element.225) | copy-start | bytes 147460
  58.2 7.5 %copy-start.12 = (f32[1,3,16,256]{3,2,1,0:T(8,128)S(1)}, f32[1,3,16,256]{3,2,1,0:T(8,128)}, u32[]{:S(2)}) copy-start(f32[1,3,16,256]{3,2,1,0:T(8,128)} %get-tuple-element.223) | copy-start | bytes 147460
  58.2 9.8 %copy-start.11 = (f32[1,3,16,256]{3,2,1,0:T(8,128)S(1)}, f32[1,3,16,256]{3,2,1,0:T(8,128)}, u32[]{:S(2)}) copy-start(f32[1,3,16,256]{3,2,1,0:T(8,128)} %get-tuple-element.219) | copy-start | bytes 147460
  58.2 10.7 %copy-start.8 = (f32[1,4,16,256]{3,2,1,0:T(8,128)S(1)}, f32[1,4,16,256]{3,2,1,0:T(8,128)}, u32[]{:S(2)}) copy-start(f32[1,4,16,256]{3,2,1,0:T(8,128)} %get-tuple-element.215) | copy-start | bytes 196612
  58.4 12.2 %copy-start.7 = (f32[1,4,16,256]{3,2,1,0:T(8,128)S(1)}, f32[1,4,16,256]{3,2,1,0:T(8,128)}, u32[]{:S(2)}) copy-start(f32[1,4,16,256]{3,2,1,0:T(8,128)} %get-tuple-element.207) | copy-start | bytes 196612
  58.5 13.4 %collective-permute-start.14 = (f32[1,64,128]{2,1,0:T(8,128)S(1)}, f32[1,64,128]{2,1,0:T(8,128)}, u32[]{:S(2)}, u32[]{:S(2)}) collective-permute-start(f32[1,64,128]{2,1,0:T(8,128)S(1)} %get-tuple-element.247), channel_id=1, source_target_pairs={{0,4},{4,8},{8,12},{12,16},{16,20},{20,24},{24,28},{28,0},{1,5},{5... | collective-permute-start | bytes 98312 | tf_op jit(solution)/shard_map/ppermute | solution.py:38
  58.6 13.3 %collective-permute-start.15 = (f32[1,64,128]{2,1,0:T(8,128)S(1)}, f32[1,64,128]{2,1,0:T(8,128)}, u32[]{:S(2)}, u32[]{:S(2)}) collective-permute-start(f32[1,64,128]{2,1,0:T(8,128)S(1)} %get-tuple-element.248), channel_id=1, source_target_pairs={{4,0},{8,4},{12,8},{16,12},{20,16},{24,20},{28,24},{0,28},{5,1},{9... | collective-permute-start | bytes 98312 | tf_op jit(solution)/shard_map/ppermute | solution.py:41
  72.8 11.6 %copy-start.20 = (f32[4,128]{1,0:T(4,128)S(1)}, f32[4,128]{1,0:T(4,128)}, u32[]{:S(2)}) copy-start(f32[4,128]{1,0:T(4,128)} %copy-done.19) | copy-start | bytes 6148
  72.8 7.2 %collective-permute-start.16 = (f32[6,64,1]{2,1,0:T(8,128)S(1)}, f32[6,64,1]{2,1,0:T(8,128)S(1)}, u32[]{:S(2)}, u32[]{:S(2)}) collective-permute-start(f32[6,64,1]{2,1,0:T(8,128)S(1)} %get-tuple-element.241), channel_id=1, source_target_pairs={{0,1},{1,2},{2,3},{3,0},{4,5},{5,6},{6,7},{7,4},{8,9},{9,10},{10,1... | collective-permute-start | bytes 4616 | tf_op jit(solution)/shard_map/ppermute | solution.py:38
  72.9 10.4 %collective-permute-start.17 = (f32[6,64,1]{2,1,0:T(8,128)S(1)}, f32[6,64,1]{2,1,0:T(8,128)S(1)}, u32[]{:S(2)}, u32[]{:S(2)}) collective-permute-start(f32[6,64,1]{2,1,0:T(8,128)S(1)} %get-tuple-element.242), channel_id=1, source_target_pairs={{1,0},{2,1},{3,2},{0,3},{5,4},{6,5},{7,6},{4,7},{9,8},{10,9},{11,1... | collective-permute-start | bytes 4616 | tf_op jit(solution)/shard_map/ppermute | solution.py:41
  83.3 6.1 %copy-start.3 = (f32[3,16,256]{2,0,1:T(4,128)S(1)}, f32[3,16,256]{2,0,1:T(4,128)}, u32[]{:S(2)}) copy-start(f32[3,16,256]{2,0,1:T(4,128)} %get-tuple-element.300) | copy-start | bytes 147460
  84.3 4.1 %copy-start.33 = (f32[5,4,16,1]{2,1,3,0:T(4,128)S(1)}, f32[5,4,16,1]{2,1,3,0:T(4,128)}, u32[]{:S(2)}) copy-start(f32[5,4,16,1]{2,1,3,0:T(4,128)} %constant_dynamic-update-slice_fusion.9) | copy-start | bytes 3844
  84.3 4.1 %copy-start.26 = (f32[4,16,1]{1,0,2:T(4,128)S(1)}, f32[4,16,1]{1,0,2:T(4,128)}, u32[]{:S(2)}) copy-start(f32[4,16,1]{1,0,2:T(4,128)} %copy.156) | copy-start | bytes 772
  84.3 4.1 %copy-start.25 = (f32[4,16,1]{1,0,2:T(4,128)S(1)}, f32[4,16,1]{1,0,2:T(4,128)}, u32[]{:S(2)}) copy-start(f32[4,16,1]{1,0,2:T(4,128)} %copy.158) | copy-start | bytes 772
  84.3 4.7 %copy-start.34 = (f32[5,4,16,1]{2,1,3,0:T(4,128)S(1)}, f32[5,4,16,1]{2,1,3,0:T(4,128)}, u32[]{:S(2)}) copy-start(f32[5,4,16,1]{2,1,3,0:T(4,128)} %constant_dynamic-update-slice_fusion.4) | copy-start | bytes 3844
  84.3 4.7 %copy-start.24 = (f32[4,16,1]{1,0,2:T(4,128)S(1)}, f32[4,16,1]{1,0,2:T(4,128)}, u32[]{:S(2)}) copy-start(f32[4,16,1]{1,0,2:T(4,128)} %copy.147) | copy-start | bytes 772
  84.3 4.7 %copy-start.23 = (f32[4,16]{1,0:T(4,128)S(1)}, f32[4,16]{1,0:T(4,128)}, u32[]{:S(2)}) copy-start(f32[4,16]{1,0:T(4,128)} %slice_reduce_fusion) | copy-start | bytes 772
  84.3 5.0 %copy-start.31 = (f32[5,4,1,256]{3,1,2,0:T(4,128)S(1)}, f32[5,4,1,256]{3,1,2,0:T(4,128)}, u32[]{:S(2)}) copy-start(f32[5,4,1,256]{3,1,2,0:T(4,128)} %constant_dynamic-update-slice_fusion.19) | copy-start | bytes 61444
  84.3 5.1 %copy-start.4 = (f32[3,16,256]{2,0,1:T(4,128)S(1)}, f32[3,16,256]{2,0,1:T(4,128)}, u32[]{:S(2)}) copy-start(f32[3,16,256]{2,0,1:T(4,128)} %get-tuple-element.301) | copy-start | bytes 147460
  84.3 7.9 %copy-start.6 = (f32[4,16,255]{2,0,1:T(4,128)S(1)}, f32[4,16,255]{2,0,1:T(4,128)}, u32[]{:S(2)}) copy-start(f32[4,16,255]{2,0,1:T(4,128)} %slice.1057) | copy-start | bytes 195844
  86.6 9.7 %copy-start.27 = (s32[4,256]{1,0:T(4,128)S(1)}, s32[4,256]{1,0:T(4,128)}, u32[]{:S(2)}) copy-start(s32[4,256]{1,0:T(4,128)} %param.44) | copy-start | bytes 12292
  86.6 9.7 %copy-start.28 = (s32[4,256]{1,0:T(4,128)S(1)}, s32[4,256]{1,0:T(4,128)}, u32[]{:S(2)}) copy-start(s32[4,256]{1,0:T(4,128)} %param.43) | copy-start | bytes 12292
  86.7 9.7 %copy-start.10 = (f32[4,15,256]{2,0,1:T(4,128)S(1)}, f32[4,15,256]{2,0,1:T(4,128)}, u32[]{:S(2)}) copy-start(f32[4,15,256]{2,0,1:T(4,128)} %slice.1086) | copy-start | bytes 184324
  88.4 1.2 %collective-permute-start.3 = (f32[5,4,16,1]{2,1,3,0:T(4,128)S(1)}, f32[5,4,16,1]{2,1,3,0:T(4,128)S(1)}, u32[]{:S(2)}, u32[]{:S(2)}) collective-permute-start(f32[5,4,16,1]{2,1,3,0:T(4,128)S(1)} %constant_dynamic-update-slice_fusion.5), channel_id=1, source_target_pairs={{0,2},{2,0},{1,3},{3,1},{4,6},{6,4},{5,7},{7,5},{8,10},{10,8},{9,1... | collective-permute-start | bytes 3848 | tf_op jit(solution)/shard_map/ppermute | solution.py:23
  89.1 1.2 %collective-permute-start.2 = (f32[5,4,16,1]{2,1,3,0:T(4,128)S(1)}, f32[5,4,16,1]{2,1,3,0:T(4,128)S(1)}, u32[]{:S(2)}, u32[]{:S(2)}) collective-permute-start(f32[5,4,16,1]{2,1,3,0:T(4,128)S(1)} %constant_dynamic-update-slice_fusion), channel_id=1, source_target_pairs={{0,2},{2,0},{1,3},{3,1},{4,6},{6,4},{5,7},{7,5},{8,10},{10,8},{9,1... | collective-permute-start | bytes 3848 | tf_op jit(solution)/shard_map/ppermute | solution.py:23
  90.6 5.7 %collective-permute-start.5 = (f32[5,4,1,256]{3,1,2,0:T(4,128)S(1)}, f32[5,4,1,256]{3,1,2,0:T(4,128)S(1)}, u32[]{:S(2)}, u32[]{:S(2)}) collective-permute-start(f32[5,4,1,256]{3,1,2,0:T(4,128)S(1)} %constant_dynamic-update-slice_fusion.15), channel_id=1, source_target_pairs={{1,0},{3,2},{5,4},{7,6},{9,8},{11,10},{13,12},{15,14},{17,16},{19,... | collective-permute-start | bytes 61448 | tf_op jit(solution)/shard_map/ppermute | solution.py:29
  92.2 10.1 %copy-start.9 = (f32[4,15,256]{2,0,1:T(4,128)S(1)}, f32[4,15,256]{2,0,1:T(4,128)}, u32[]{:S(2)}) copy-start(f32[4,15,256]{2,0,1:T(4,128)} %slice.1083) | copy-start | bytes 184324
  97.3 3.1 %collective-permute-start.4 = (f32[5,4,1,256]{3,2,1,0:T(1,128)S(1)}, f32[5,4,1,256]{3,2,1,0:T(1,128)S(1)}, u32[]{:S(2)}, u32[]{:S(2)}) collective-permute-start(f32[5,4,1,256]{3,2,1,0:T(1,128)S(1)} %copy.165), channel_id=1, source_target_pairs={{0,1},{2,3},{4,5},{6,7},{8,9},{10,11},{12,13},{14,15},{16,17},{18,... | collective-permute-start | bytes 61448 | tf_op jit(solution)/shard_map/ppermute | solution.py:29
  (5 other events, 10.0 us)
where the time goes:
time: 106 us; the launch traced here: 105 us
  waiting for transfers between devices  28.2 us (27%)
  local copies, waits for them, and re-layouts  27.6 us (26%)
  starting transfers between devices  26.7 us (25%)
  other arithmetic  10.6 us (10%)
  matrix products  5.46 us (5%)
  blocking collectives  4.95 us (5%)
  between operations  1.72 us (2%)
    ppermute x6, starting transfers between devices, padded(): lax.ppermute(lax.slice_in_dim(block, 0, width, axis=dim), axis, backward)  14.2 us
    ppermute x6, waiting for transfers between devices, padded(): lax.ppermute(lax.slice_in_dim(block, 0, width, axis=dim), axis, backward)  12.5 us
    ppermute x6, waiting for transfers between devices, padded(): lax.ppermute(lax.slice_in_dim(block, block.shape[dim] - width, None, axis...  10.3 us
    unnamed x119, local copies, waits for them, and re-layouts  7.07 us
    ppermute x6, starting transfers between devices, padded(): lax.ppermute(lax.slice_in_dim(block, block.shape[dim] - width, None, axis...  6.87 us
    psum x1, blocking collectives, broadcast(): return lax.psum(block, axis)  4.95 us
    ppermute x2, waiting for transfers between devices, from_behind(): return lax.ppermute(block, axis, route)  4.62 us
    slice x3, local copies, waits for them, and re-layouts, padded(): lax.slice_in_dim(block, 0, width, axis=dim)  3.01 us
  transfers between devices with their start and end apart: 18, of which 10 were waited for; matrix products, arithmetic and copies ran while one was open for 33% of the time, Pallas kernels for 0%

commit v1 on v0

v1 whole, which is shorter than its diff:
```python
import functools
import jax
import jax.numpy as jnp
import numpy as np
from jax import lax
from jax.experimental import pallas as pl
from jax.experimental.pallas import tpu as pltpu
from jax.sharding import PartitionSpec as P

JET_SPEED = 0.1
H_BASE = 0.5
H_GAIN = 40.0
LANES = 128
ROWS = 8
MESH = pl.DeviceIdType.MESH

VELOCITIES = [
    (0, 0, 0),
    (1, 0, 0), (-1, 0, 0), (0, 1, 0), (0, -1, 0), (0, 0, 1), (0, 0, -1),
    (1, 1, 0), (-1, -1, 0), (1, -1, 0), (-1, 1, 0),
    (1, 0, 1), (-1, 0, -1), (1, 0, -1), (-1, 0, 1),
    (0, 1, 1), (0, -1, -1), (0, 1, -1), (0, -1, 1),
]
COUNT = len(VELOCITIES)
WEIGHTS = [1.0 / 3.0] + [1.0 / 18.0] * 6 + [1.0 / 36.0] * 12
INDEX = {velocity: member for member, velocity in enumerate(VELOCITIES)}
OPPOSITE = [INDEX[(-a, -b, -c)] for a, b, c in VELOCITIES]
ORDER = [i for s in (1, -1, 0) for i in range(COUNT) if VELOCITIES[i][0] == s]
SLOT = {member: place for place, member in enumerate(ORDER)}
FACE = sum(1 for v in VELOCITIES if v[0] == 1)
ACROSS = [(0, 0), (1, 0), (-1, 0), (0, 1), (0, -1)]


def collide(f):
    s = {i: f[i] + f[i + 1] for i in range(1, COUNT, 2)}
    d = {i: f[i] - f[i + 1] for i in range(1, COUNT, 2)}
    jx = (d[1] + d[7]) + (d[9] + d[11]) + d[13]
    jy = (d[3] + d[7]) + (d[15] - d[9]) + d[17]
    jz = (d[5] + d[11]) + (d[15] - d[13]) - d[17]
    sxy, sxz, syz = s[7] + s[9], s[11] + s[13], s[15] + s[17]
    rho = f[0] + (s[1] + s[3] + s[5]) + (sxy + sxz + syz)
    inv = 1.0 / rho
    ux, uy, uz = jx * inv, jy * inv, jz * inv
    px, py, pz = jx * ux, jy * uy, jz * uz
    p = px + py + pz
    base = rho - 1.5 * p
    hxy, hxz, hyz = px + py, px + pz, py + pz
    c4 = 4.0 * f[0] - base
    qxy = c4 + sxy - 2.0 * (s[1] + s[3]) + 0.5 * hxy
    qxz = c4 + sxz - 2.0 * (s[1] + s[5]) + 0.5 * hxz
    qyz = c4 + syz - 2.0 * (s[3] + s[5]) + 0.5 * hyz
    mean = (qxy + qxz + qyz) * (2.0 / 7.0)
    txy, txz, tyz = ((q - mean) * (0.2 / 12.0) for q in (qxy, qxz, qyz))
    post = [None] * COUNT
    post[0] = (1.6 / 3.0) * base - 0.6 * f[0] + 4.0 * (txy + txz + tyz)
    axis_base = (1.6 / 18.0) * base
    for i, pp, tt, j in ((1, px, txy + txz, jx), (3, py, txy + tyz, jy), (5, pz, txz + tyz, jz)):
        even = axis_base + 0.4 * pp - 0.3 * s[i] - 2.0 * tt
        odd = 0.2 * j - 0.1 * d[i]
        post[i], post[i + 1] = even + odd, even - odd
    diag_base = (1.6 / 36.0) * base
    for i, hh, tt, j, k, u in (
        (7, hxy, txy, jx, jy, uy), (11, hxz, txz, jx, jz, uz), (15, hyz, tyz, jy, jz, uz)
    ):
        both = diag_base + 0.2 * hh + tt
        cross = 0.4 * (j * u)
        even = both + cross - 0.3 * s[i]
        odd = 0.1 * (j + k - d[i])
        post[i], post[i + 1] = even + odd, even - odd
        even = both - cross - 0.3 * s[i + 2]
        odd = 0.1 * (j - k - d[i + 2])
        post[i + 2], post[i + 3] = even + odd, even - odd
    return post, p * inv


def lanes_like(shape):
    return lax.broadcasted_iota(jnp.int32, shape, len(shape) - 1)


def rows_like(shape):
    return lax.broadcasted_iota(jnp.int32, shape, len(shape) - 2)


def turned(value, shift, axis):
    shift = shift % value.shape[axis]
    return value if shift == 0 else pltpu.roll(value, shift, axis)


def edge_pack(tiles, last):
    lane = lanes_like((ROWS, LANES))
    packed = jnp.zeros((ROWS, LANES), jnp.float32)
    for k, tile in enumerate(tiles):
        packed = jnp.where(lane == k, turned(tile, k + 1 if last else k, 1), packed)
    return packed


def edge_column(packed, places, last):
    return jnp.concatenate(
        [turned(packed, (LANES - 1 if last else 0) - k, 1) for k in places], axis=0
    )


def kernel(sizes, pops_ref, temp_ref, diff_ref, nozzle_ref, wall_ref, load_ref, cool_ref,
           out_ref, solid_ref, pops, post, temp, diff, first, links, base, inverse, heat,
           sx_in, sy_out, sy_in, heat_out, heat_in, px_in, py_out, py_in, pz_out, pz_in,
           xy_in, xz_out, xz_in, yz_out, yz_in, fx_in, fy_out, fy_in,
           load_sem, send_sem, recv_sem):
    nx, ny, nz = sizes
    gx, gy, gz = (lax.axis_index(name) for name in ("gx", "gy", "gz"))
    X, Z, Y = pops.shape[1:]
    D, W = temp.shape[1:]
    lowest = gz == 0

    def device(dx, dy, other):
        return (lax.rem(gx + dx + nx, nx), lax.rem(gy + dy + ny, ny), 1 - gz if other else gz)

    ahead = (gx, lax.rem(gy + gz, ny), 1 - gz)
    behind = (gx, lax.rem(gy + gz - 1 + ny, ny), 1 - gz)

    near = set()
    for dx, dy, other in (
        [(s, 0, 0) for s in (1, -1)] + [(0, s, 0) for s in (1, -1)] + [(0, 0, 1)]
        + [(s, t, 0) for s in (1, -1) for t in (1, -1)]
        + [(s, 0, 1) for s in (1, -1)] + [(0, s, 1) for s in (1, -1)]
    ):
        near.add((dx % nx, dy % ny, other))
    barrier = pltpu.get_barrier_semaphore()
    for dx, dy, other in sorted(near):
        pl.semaphore_signal(
            barrier, inc=1, device_id=device(dx, dy, other), device_id_type=MESH
        )

    loads = [
        pltpu.make_async_copy(temp_ref, temp, load_sem.at[X]),
        pltpu.make_async_copy(diff_ref, diff, load_sem.at[X + 1]),
    ]
    for copy in loads:
        copy.start()
    turn = [X - 1] + list(range(X - 1))
    for x in turn:
        pltpu.make_async_copy(pops_ref.at[:, x], pops.at[:, x], load_sem.at[x]).start()

    sent = []

    def send(source, target, where):
        place = len(sent)
        copy = pltpu.make_async_remote_copy(
            src_ref=source, dst_ref=target, send_sem=send_sem.at[place],
            recv_sem=recv_sem.at[place], device_id=where, device_id_type=MESH,
        )
        copy.start()
        sent.append(copy)
        return copy

    def blocks(ref):
        return [ref[x, z:z + ROWS, :] for x in range(X) for z in range(0, D, ROWS)]

    depth_blocks = D // ROWS
    for copy in loads:
        copy.wait()
    halved = [0.5 * tile for tile in blocks(diff)]
    sy_out[0] = edge_pack(blocks(temp) + halved, True)
    sy_out[1] = edge_pack(blocks(temp) + halved, False)
    pl.semaphore_wait(barrier, len(near))
    sink_in = []
    for side, (edge, dx) in enumerate(((X - 1, 1), (0, -1))):
        sink_in.append(send(temp.at[edge], sx_in.at[side, 0], device(dx, 0, 0)))
        sink_in.append(send(diff.at[edge], sx_in.at[side, 1], device(dx, 0, 0)))
    sink_in.append(send(sy_out.at[0], sy_in.at[0], ahead))
    sink_in.append(send(sy_out.at[1], sy_in.at[1], behind))

    def collide_plane(step, carry):
        x = lax.rem(step + X - 1, X)
        pltpu.make_async_copy(pops_ref.at[:, x], pops.at[:, x], load_sem.at[x]).wait()
        for z in range(0, Z, ROWS):
            for y in range(0, Y, LANES):
                tile = [pops[i, x, z:z + ROWS, y:y + LANES] for i in range(COUNT)]
                done, square = collide(tile)
                for i in range(COUNT):
                    post[SLOT[i], x, z:z + ROWS, y:y + LANES] = done[i]
                if z == 0:
                    heat[x, :, y:y + LANES] = H_BASE + H_GAIN * square
        return carry

    lax.fori_loop(0, 2, collide_plane, 0)
    face_in, edge_in = [], []
    for side, (edge, dx) in enumerate(((X - 1, 1), (0, -1))):
        face_in.append(
            send(post.at[pl.ds(side * FACE, FACE), edge], px_in.at[side], device(dx, 0, 0))
        )
    for side, (edge, dx) in enumerate(((X - 1, 1), (0, -1))):
        for flank, (lane, dy) in enumerate(((Y - LANES, 1), (0, -1))):
            member = SLOT[INDEX[(dx, dy, 0)]]
            edge_in.append(send(
                post.at[member, edge, :, pl.ds(lane, LANES)], xy_in.at[side, flank],
                device(dx, dy, 0),
            ))
    lax.fori_loop(2, X, collide_plane, 0)

    for x in range(X):
        heat_out[x:x + 1, :] = heat[x, 0:1, W:2 * W]
    heat_copy = send(heat_out, heat_in, device(0, 0, 1))

    for side, (lane, dy) in enumerate(((Y - LANES, 1), (0, -1))):
        tiles = [
            post[SLOT[INDEX[(a, dy, c)]], x, z:z + ROWS, lane:lane + LANES]
            for a, c in ACROSS for x in range(X) for z in range(0, Z, ROWS)
        ]
        py_out[side] = edge_pack(tiles, dy == 1)
        edge_in.append(send(py_out.at[side], py_in.at[side], device(0, dy, 0)))
    for k, (a, b) in enumerate(ACROSS):
        for x in range(X):
            row = jnp.where(
                lowest,
                post[SLOT[INDEX[(a, b, 1)]], x, Z - 1:Z, :],
                post[SLOT[INDEX[(a, b, -1)]], x, 0:1, :],
            )
            pz_out[k * X + x:k * X + x + 1, :] = row
            if (a, x) in ((1, X - 1), (-1, 0)):
                xz_out[0 if a == 1 else 1, 0:1, :] = row
            if b == 1:
                yz_out[0, x:x + 1, :] = row[:, Y - LANES:]
            if b == -1:
                yz_out[1, x:x + 1, :] = row[:, :LANES]
    edge_in.append(send(pz_out, pz_in, device(0, 0, 1)))
    for side, s in enumerate((1, -1)):
        edge_in.append(send(xz_out.at[side], xz_in.at[side], device(s, 0, 1)))
        edge_in.append(send(yz_out.at[side], yz_in.at[side], device(0, s, 1)))

    lane = lanes_like((D, W))
    depth = rows_like((D, W))
    column = depth_blocks * X

    def beside(value, packs, x, start):
        places = range(start + x * depth_blocks, start + (x + 1) * depth_blocks)
        low = jnp.where(lane == 0, edge_column(packs[0], places, False), turned(value, 1, 1))
        high = jnp.where(
            lane == W - 1, edge_column(packs[1], places, True), turned(value, -1, 1)
        )
        return low, high

    for copy in sink_in:
        copy.wait_recv()
    heat_copy.wait_recv()
    packs = (sy_in[0], sy_in[1])
    for x in range(X):
        own, cond = temp[x], 0.5 * diff[x]
        below = (temp[x - 1], diff[x - 1]) if x > 0 else (sx_in[0, 0], sx_in[0, 1])
        above = (temp[x + 1], diff[x + 1]) if x < X - 1 else (sx_in[1, 0], sx_in[1, 1])
        temps = [below[0], above[0], *beside(own, packs, x, 0)]
        conds = [0.5 * below[1], 0.5 * above[1], *beside(cond, packs, x, column)]
        g = [cond + c for c in conds]
        g.append(jnp.where(depth == D - 1, 0.0, cond + turned(cond, -1, 0)))
        g.append(jnp.where(depth == 0, 0.0, cond + turned(cond, 1, 0)))
        temps += [turned(own, -1, 0), turned(own, 1, 0)]
        warm = jnp.where(lowest, heat[x, 0:1, 0:W], heat_in[x:x + 1, :])
        start = own + jnp.where(depth == 0, load_ref[x:x + 1, :], 0.0)
        start = start + jnp.where(depth == D - 1, warm * cool_ref[x:x + 1, :], 0.0)
        denom = 1.0 + jnp.where(depth == D - 1, warm, 0.0)
        numer = start
        for k in range(6):
            numer = numer + g[k] * temps[k]
            denom = denom + g[k]
            links[k, x] = g[k]
        flip = 1.0 / denom
        base[x] = start
        inverse[x] = flip
        first[x] = numer * flip
    first_in = []
    for side, (edge, dx) in enumerate(((X - 1, 1), (0, -1))):
        first_in.append(send(first.at[edge], fx_in.at[side], device(dx, 0, 0)))
    fy_out[0] = edge_pack(blocks(first), True)
    first_in.append(send(fy_out.at[0], fy_in.at[0], ahead))
    fy_out[1] = edge_pack(blocks(first), False)
    first_in.append(send(fy_out.at[1], fy_in.at[1], behind))

    wide = lanes_like((Z, Y))
    flat = lanes_like((1, Y))
    level = rows_like((Z, Y))

    def shifted(value, lanes, border, b):
        parts = [border, value[:, LANES:]] if b == 1 else [value[:, :Y - LANES], border]
        edge = jnp.concatenate(parts, axis=1)
        spot = 0 if b == 1 else Y - 1
        return jnp.where(lanes == spot, edge, turned(value, b, 1))

    for copy in edge_in:
        copy.wait_recv()
    tall = Z // ROWS
    py_packs = (py_in[0], py_in[1])

    def assemble(x):
        height_rows = {}
        for k, (a, b) in enumerate(ACROSS):
            source = x - a
            if 0 <= source < X:
                row = pz_in[k * X + source:k * X + source + 1, :]
            else:
                row = xz_in[0 if a == 1 else 1, 0:1, :]
            if b != 0:
                flank = 0 if b == 1 else 1
                border = turned(yz_in[flank], b, 1)[x:x + 1, :]
                row = shifted(row, flat, border, b)
            height_rows[(a, b)] = row
        nozzle = nozzle_ref[x:x + 1, :] == 1
        outlet = wall_ref[x:x + 1, :] == 1
        for i, (a, b, c) in enumerate(VELOCITIES):
            source = x - a
            side = 0 if a == 1 else 1
            inside = 0 <= source < X
            value = post[SLOT[i], source] if inside else px_in[side, SLOT[i] - side * FACE]
            if b != 0:
                flank = 0 if b == 1 else 1
                if inside:
                    begin = (ACROSS.index((a, c)) * X + source) * tall
                    border = edge_column(
                        py_packs[flank], range(begin, begin + tall), b == -1
                    )
                else:
                    border = turned(xy_in[side, flank], b, 1)
                value = shifted(value, wide, border, b)
            if c != 0:
                value = turned(value, c, 0)
                back = SLOT[OPPOSITE[i]]
                if c == 1:
                    row = jnp.where(lowest, post[back, x, 0:1, :], height_rows[(a, b)])
                    value = jnp.where(level == 0, row, value)
                else:
                    closed = post[back, x, Z - 1:Z, :]
                    jet = closed + 6.0 * WEIGHTS[i] * JET_SPEED
                    plate = jnp.where(
                        nozzle, jet, jnp.where(outlet, post[SLOT[i], x, Z - 1:Z, :], closed)
                    )
                    row = jnp.where(lowest, height_rows[(a, b)], plate)
                    value = jnp.where(level == Z - 1, row, value)
            out_ref[i, x] = value

    for x in range(1, X - 1):
        assemble(x)
    for copy in face_in:
        copy.wait_recv()
    assemble(0)
    assemble(X - 1)

    for copy in first_in:
        copy.wait_recv()
    packs = (fy_in[0], fy_in[1])
    for x in range(X):
        own = first[x]
        below = first[x - 1] if x > 0 else fx_in[0]
        above = first[x + 1] if x < X - 1 else fx_in[1]
        temps = [below, above, *beside(own, packs, x, 0), turned(own, -1, 0), turned(own, 1, 0)]
        numer = base[x]
        for k in range(6):
            numer = numer + links[k, x] * temps[k]
        solid_ref[x] = numer * inverse[x]
    for copy in sent:
        copy.wait_send()


def body(populations, nozzle_mask, wall_type, solid_temp, diffusion, heat_load, coolant_temp):
    sizes = tuple(lax.axis_size(name) for name in ("gx", "gy", "gz"))
    assert sizes[0] > 1 and sizes[1] > 1 and sizes[2] == 2
    _, X, Z, Y = populations.shape
    _, D, W = solid_temp.shape
    assert X >= 2 and W == LANES and Y == sizes[2] * W and Z % ROWS == 0 and D % ROWS == 0
    assert 2 * X * (D // ROWS) <= LANES and len(ACROSS) * X * (Z // ROWS) <= LANES
    rows = -(-len(ACROSS) * X // ROWS) * ROWS
    tall = -(-X // ROWS) * ROWS

    def vmem(*shape):
        return pltpu.VMEM(shape, jnp.float32)

    pair = vmem(2, ROWS, LANES)
    scratch = [
        vmem(COUNT, X, Z, Y), vmem(COUNT, X, Z, Y),
        vmem(X, D, W), vmem(X, D, W), vmem(X, D, W),
        vmem(6, X, D, W), vmem(X, D, W), vmem(X, D, W),
        vmem(X, ROWS, Y),
        vmem(2, 2, D, W), pair, pair,
        vmem(tall, W), vmem(tall, W),
        vmem(2, FACE, Z, Y), pair, pair,
        vmem(rows, Y), vmem(rows, Y),
        vmem(2, 2, Z, LANES), vmem(2, ROWS, Y), vmem(2, ROWS, Y),
        vmem(2, tall, LANES), vmem(2, tall, LANES),
        vmem(2, D, W), pair, pair,
        pltpu.SemaphoreType.DMA((X + 2,)),
        pltpu.SemaphoreType.DMA((24,)),
        pltpu.SemaphoreType.DMA((24,)),
    ]
    anywhere = pl.BlockSpec(memory_space=pl.ANY)
    local = pl.BlockSpec(memory_space=pltpu.VMEM)
    return pl.pallas_call(
        functools.partial(kernel, sizes),
        out_shape=OUTS(populations, solid_temp),
        in_specs=[anywhere] * 3 + [local] * 4,
        out_specs=[local, local],
        scratch_shapes=scratch,
        compiler_params=pltpu.CompilerParams(
            collective_id=0, has_side_effects=True, vmem_limit_bytes=24 * 1024 * 1024
        ),
    )(populations, solid_temp, diffusion, nozzle_mask, wall_type, heat_load, coolant_temp)


def OUTS(populations, solid_temp):
    return (
        pltpu.VMEM(populations.shape, jnp.float32),
        pltpu.VMEM(solid_temp.shape, jnp.float32),
    )


def solution(mesh):
    placed = (
        P(None, "gx", "gz", "gy"),
        P("gx", "gy"),
        P("gx", "gy"),
        P("gx", None, ("gy", "gz")),
        P("gx", None, ("gy", "gz")),
        P("gx", ("gy", "gz")),
        P("gx", ("gy", "gz")),
    )
    return jax.shard_map(
        body,
        mesh=mesh,
        in_specs=placed,
        out_specs=(P(None, "gx", "gz", "gy"), P("gx", None, ("gy", "gz"))),
        check_vma=False,
    )
```

time: 106 us -> 26.2 us (0.25)
  waiting for transfers between devices: 28.2 us -> 0 us
  starting transfers between devices: 26.7 us -> 0 us
  local copies, waits for them, and re-layouts: 27.6 us -> 7.52 us
  Pallas kernels: 0 us -> 17.7 us
  other arithmetic: 10.6 us -> 0 us
  matrix products: 5.46 us -> 0 us
  blocking collectives: 4.95 us -> 0 us
  between operations: 1.72 us -> 0.66 us
    ppermute x18 -> x0, waiting for transfers between devices: 28.2 us -> none  [the longest x6 12.5 us: padded(): lax.ppermute(lax.slice_in_dim(block, 0, width, axis=dim), axis, backward)]
    ppermute x18 -> x0, starting transfers between devices: 26.7 us -> none  [the longest x6 14.2 us: padded(): lax.ppermute(lax.slice_in_dim(block, 0, width, axis=dim), axis, backward)]
    pallas_call x0 -> x1, Pallas kernels: none -> 17.7 us  [body(): pl.pallas_call(functools.partial(kernel, sizes), out_shape=OUTS(populatio...]
    slice x33 -> x0, local copies, waits for them, and re-layouts: 13.2 us -> none  [the longest x3 3.01 us: padded(): lax.slice_in_dim(block, 0, width, axis=dim)]
    dot_general x3 -> x0, matrix products: 5.46 us -> none  [the longest x1 2.28 us: collide(): jnp.einsum('pq,qxzy->pxzy', jnp.asarray(relax_table()), pops - equil, pre...]
    psum x1 -> x0, blocking collectives: 4.95 us -> none  [broadcast(): return lax.psum(block, axis)]
    squeeze x19 -> x0, local copies, waits for them, and re-layouts: 4.57 us -> none  [the longest x8 1.84 us: body(): up_plane[position]]
    scatter x5 -> x0, other arithmetic: 2.15 us -> none  [the longest x4 2.14 us: apply_walls(): layer.at[:, -1, :].set(jnp.where(at_top, top_value, layer[:, -1, :]))]
  transfers between devices with their start and end apart: 18 -> 0, of which waited for: 10 -> 0; matrix products, arithmetic and copies ran while one was open for 33% -> 0% of each run, Pallas kernels for 0% -> 0%
where the time goes in v1:
time: 26.2 us; the launch traced here: 25.9 us
  Pallas kernels  17.7 us (68%)
  local copies, waits for them, and re-layouts  7.52 us (29%)
  between operations  0.66 us (3%)
    pallas_call x1, Pallas kernels, body(): pl.pallas_call(functools.partial(kernel, sizes), out_shape=OUTS(populatio...  17.7 us
    unnamed x16, local copies, waits for them, and re-layouts  7.52 us

profile of v1, /device:TPU:0, one launch (start us, length us, event | category | flops | bytes accessed | tf_op | source)
XLA Modules:
  0.0 25.9 jit_solution(6188149635957582581)
XLA Ops:
  0.6 0.0 copy-start
  0.6 1.3 %copy-done = f32[19,4,16,256]{3,2,1,0:T(8,128)S(1)} copy-done((f32[19,4,16,256]{3,2,1,0:T(8,128)S(1)}, f32[19,4,16,256]{3,2,1,0:T(8,128)}, u32[]{:S(2)}) %copy-start) | copy-done | bytes 1245208
  1.9 0.0 copy-start.1
  1.9 0.9 %copy-done.1 = f32[4,64,128]{2,1,0:T(8,128)S(1)} copy-done((f32[4,64,128]{2,1,0:T(8,128)S(1)}, f32[4,64,128]{2,1,0:T(8,128)}, u32[]{:S(2)}) %copy-start.1) | copy-done | bytes 131096
  2.8 0.0 copy-start.2
  2.8 0.9 %copy-done.2 = f32[4,64,128]{2,1,0:T(8,128)S(1)} copy-done((f32[4,64,128]{2,1,0:T(8,128)S(1)}, f32[4,64,128]{2,1,0:T(8,128)}, u32[]{:S(2)}) %copy-start.2) | copy-done | bytes 131096
  3.7 0.0 copy-start.3
  3.7 0.7 %copy-done.3 = s32[4,256]{1,0:T(4,128)S(1)} copy-done((s32[4,256]{1,0:T(4,128)S(1)}, s32[4,256]{1,0:T(4,128)}, u32[]{:S(2)}) %copy-start.3) | copy-done | bytes 4120
  4.4 0.0 copy-start.4
  4.4 0.7 %copy-done.4 = s32[4,256]{1,0:T(4,128)S(1)} copy-done((s32[4,256]{1,0:T(4,128)S(1)}, s32[4,256]{1,0:T(4,128)}, u32[]{:S(2)}) %copy-start.4) | copy-done | bytes 4120
  5.1 0.0 copy-start.5
  5.1 0.7 %copy-done.5 = f32[4,128]{1,0:T(4,128)S(1)} copy-done((f32[4,128]{1,0:T(4,128)S(1)}, f32[4,128]{1,0:T(4,128)}, u32[]{:S(2)}) %copy-start.5) | copy-done | bytes 2072
  5.8 0.0 copy-start.6
  5.8 0.7 %copy-done.6 = f32[4,128]{1,0:T(4,128)S(1)} copy-done((f32[4,128]{1,0:T(4,128)S(1)}, f32[4,128]{1,0:T(4,128)}, u32[]{:S(2)}) %copy-start.6) | copy-done | bytes 2072
  6.5 17.7 %shard_map.86 = (f32[19,4,16,256]{3,2,1,0:T(8,128)S(1)}, f32[4,64,128]{2,1,0:T(8,128)S(1)}) custom-call(f32[19,4,16,256]{3,2,1,0:T(8,128)S(1)} %copy-done, f32[4,64,128]{2,1,0:T(8,128)S(1)} %copy-done.1, f32[4,64,128]{2,1,0:T(8,128)S(1)} %copy-done.2, s32[4,256]{1,0:T(4,128)S(1)} %copy-done.3, s32[4,256]{1,0:T(4,128)S(1)} %copy-done.4, ...), custom_call_target="tpu_custom_call" | custom-call | tf_op jit(solution)/shard_map/pallas_call | solution.py:393
  24.2 1.0 %copy.11 = f32[19,4,16,256]{3,2,1,0:T(8,128)} copy(f32[19,4,16,256]{3,2,1,0:T(8,128)S(1)} %get-tuple-element.2) | data formatting | bytes 2490368
  25.2 0.7 %copy.12 = f32[4,64,128]{2,1,0:T(8,128)} copy(f32[4,64,128]{2,1,0:T(8,128)S(1)} %get-tuple-element.3) | data formatting | bytes 262144
Async XLA Ops:
  0.6 1.3 %copy-start = (f32[19,4,16,256]{3,2,1,0:T(8,128)S(1)}, f32[19,4,16,256]{3,2,1,0:T(8,128)}, u32[]{:S(2)}) copy-start(f32[19,4,16,256]{3,2,1,0:T(8,128)} %pops_ref.1) | copy-start | bytes 3735556
  1.9 0.9 %copy-start.1 = (f32[4,64,128]{2,1,0:T(8,128)S(1)}, f32[4,64,128]{2,1,0:T(8,128)}, u32[]{:S(2)}) copy-start(f32[4,64,128]{2,1,0:T(8,128)} %temp_ref.1) | copy-start | bytes 393220
  2.8 0.9 %copy-start.2 = (f32[4,64,128]{2,1,0:T(8,128)S(1)}, f32[4,64,128]{2,1,0:T(8,128)}, u32[]{:S(2)}) copy-start(f32[4,64,128]{2,1,0:T(8,128)} %diff_ref.1) | copy-start | bytes 393220
  3.7 0.7 %copy-start.3 = (s32[4,256]{1,0:T(4,128)S(1)}, s32[4,256]{1,0:T(4,128)}, u32[]{:S(2)}) copy-start(s32[4,256]{1,0:T(4,128)} %nozzle_ref.1) | copy-start | bytes 12292
  4.4 0.7 %copy-start.4 = (s32[4,256]{1,0:T(4,128)S(1)}, s32[4,256]{1,0:T(4,128)}, u32[]{:S(2)}) copy-start(s32[4,256]{1,0:T(4,128)} %wall_ref.1) | copy-start | bytes 12292
  5.1 0.7 %copy-start.5 = (f32[4,128]{1,0:T(4,128)S(1)}, f32[4,128]{1,0:T(4,128)}, u32[]{:S(2)}) copy-start(f32[4,128]{1,0:T(4,128)} %load_ref.1) | copy-start | bytes 6148
  5.8 0.7 %copy-start.6 = (f32[4,128]{1,0:T(4,128)S(1)}, f32[4,128]{1,0:T(4,128)}, u32[]{:S(2)}) copy-start(f32[4,128]{1,0:T(4,128)} %cool_ref.1) | copy-start | bytes 6148

commit v2 on v1

--- a/solution.py
+++ b/solution.py
@@ -100,8 +100,8 @@
     )
 
 
-def kernel(sizes, pops_ref, temp_ref, diff_ref, nozzle_ref, wall_ref, load_ref, cool_ref,
-           out_ref, solid_ref, pops, post, temp, diff, first, links, base, inverse, heat,
+def kernel(sizes, pops_ref, temp_ref, diff_ref, nozzle_hbm, wall_hbm, load_hbm, cool_hbm,
+           out_ref, solid_ref, nozzle_ref, wall_ref, load_ref, cool_ref, pops, post, temp, diff, first, links, base, inverse, heat,
            sx_in, sy_out, sy_in, heat_out, heat_in, px_in, py_out, py_in, pz_out, pz_in,
            xy_in, xz_out, xz_in, yz_out, yz_in, fx_in, fy_out, fy_in,
            load_sem, send_sem, recv_sem):
@@ -134,11 +134,20 @@
         pltpu.make_async_copy(temp_ref, temp, load_sem.at[X]),
         pltpu.make_async_copy(diff_ref, diff, load_sem.at[X + 1]),
     ]
+    planes = [
+        pltpu.make_async_copy(far, near_by, load_sem.at[X + 2 + k])
+        for k, (far, near_by) in enumerate((
+            (nozzle_hbm, nozzle_ref), (wall_hbm, wall_ref),
+            (load_hbm, load_ref), (cool_hbm, cool_ref),
+        ))
+    ]
     for copy in loads:
         copy.start()
     turn = [X - 1] + list(range(X - 1))
     for x in turn:
         pltpu.make_async_copy(pops_ref.at[:, x], pops.at[:, x], load_sem.at[x]).start()
+    for copy in planes:
+        copy.start()
 
     sent = []
 
@@ -155,19 +164,11 @@
     def blocks(ref):
         return [ref[x, z:z + ROWS, :] for x in range(X) for z in range(0, D, ROWS)]
 
-    depth_blocks = D // ROWS
-    for copy in loads:
-        copy.wait()
-    halved = [0.5 * tile for tile in blocks(diff)]
-    sy_out[0] = edge_pack(blocks(temp) + halved, True)
-    sy_out[1] = edge_pack(blocks(temp) + halved, False)
     pl.semaphore_wait(barrier, len(near))
     sink_in = []
     for side, (edge, dx) in enumerate(((X - 1, 1), (0, -1))):
-        sink_in.append(send(temp.at[edge], sx_in.at[side, 0], device(dx, 0, 0)))
-        sink_in.append(send(diff.at[edge], sx_in.at[side, 1], device(dx, 0, 0)))
-    sink_in.append(send(sy_out.at[0], sy_in.at[0], ahead))
-    sink_in.append(send(sy_out.at[1], sy_in.at[1], behind))
+        sink_in.append(send(temp_ref.at[edge], sx_in.at[side, 0], device(dx, 0, 0)))
+        sink_in.append(send(diff_ref.at[edge], sx_in.at[side, 1], device(dx, 0, 0)))
 
     def collide_plane(step, carry):
         x = lax.rem(step + X - 1, X)
@@ -196,6 +197,14 @@
                 device(dx, dy, 0),
             ))
     lax.fori_loop(2, X, collide_plane, 0)
+
+    for copy in loads:
+        copy.wait()
+    halved = [0.5 * tile for tile in blocks(diff)]
+    sy_out[0] = edge_pack(blocks(temp) + halved, True)
+    sink_in.append(send(sy_out.at[0], sy_in.at[0], ahead))
+    sy_out[1] = edge_pack(blocks(temp) + halved, False)
+    sink_in.append(send(sy_out.at[1], sy_in.at[1], behind))
 
     for x in range(X):
         heat_out[x:x + 1, :] = heat[x, 0:1, W:2 * W]
@@ -229,6 +238,7 @@
 
     lane = lanes_like((D, W))
     depth = rows_like((D, W))
+    depth_blocks = D // ROWS
     column = depth_blocks * X
 
     def beside(value, packs, x, start):
@@ -242,6 +252,8 @@
     for copy in sink_in:
         copy.wait_recv()
     heat_copy.wait_recv()
+    for copy in planes:
+        copy.wait()
     packs = (sy_in[0], sy_in[1])
     for x in range(X):
         own, cond = temp[x], 0.5 * diff[x]
@@ -373,6 +385,7 @@
 
     pair = vmem(2, ROWS, LANES)
     scratch = [
+        pltpu.VMEM((X, Y), jnp.int32), pltpu.VMEM((X, Y), jnp.int32), vmem(X, W), vmem(X, W),
         vmem(COUNT, X, Z, Y), vmem(COUNT, X, Z, Y),
         vmem(X, D, W), vmem(X, D, W), vmem(X, D, W),
         vmem(6, X, D, W), vmem(X, D, W), vmem(X, D, W),
@@ -384,29 +397,50 @@
         vmem(2, 2, Z, LANES), vmem(2, ROWS, Y), vmem(2, ROWS, Y),
         vmem(2, tall, LANES), vmem(2, tall, LANES),
         vmem(2, D, W), pair, pair,
-        pltpu.SemaphoreType.DMA((X + 2,)),
+        pltpu.SemaphoreType.DMA((X + 6,)),
         pltpu.SemaphoreType.DMA((24,)),
         pltpu.SemaphoreType.DMA((24,)),
     ]
-    anywhere = pl.BlockSpec(memory_space=pl.ANY)
+    far = pl.BlockSpec(memory_space=pltpu.HBM)
     local = pl.BlockSpec(memory_space=pltpu.VMEM)
-    return pl.pallas_call(
+    moved, swept = pl.pallas_call(
         functools.partial(kernel, sizes),
-        out_shape=OUTS(populations, solid_temp),
-        in_specs=[anywhere] * 3 + [local] * 4,
+        out_shape=(
+            pltpu.VMEM(populations.shape, jnp.float32),
+            pltpu.VMEM(solid_temp.shape, jnp.float32),
+        ),
+        in_specs=[far] * 7,
         out_specs=[local, local],
         scratch_shapes=scratch,
         compiler_params=pltpu.CompilerParams(
             collective_id=0, has_side_effects=True, vmem_limit_bytes=24 * 1024 * 1024
         ),
-    )(populations, solid_temp, diffusion, nozzle_mask, wall_type, heat_load, coolant_temp)
-
-
-def OUTS(populations, solid_temp):
-    return (
-        pltpu.VMEM(populations.shape, jnp.float32),
-        pltpu.VMEM(solid_temp.shape, jnp.float32),
-    )
+    )(*(
+        pltpu.with_memory_space_constraint(value, pltpu.HBM)
+        for value in (populations, solid_temp, diffusion, nozzle_mask, wall_type, heat_load,
+                      coolant_temp)
+    ))
+    return pl.pallas_call(
+        deliver,
+        out_shape=(
+            pltpu.HBM(populations.shape, jnp.float32),
+            pltpu.HBM(solid_temp.shape, jnp.float32),
+        ),
+        in_specs=[local, local],
+        out_specs=[far, far],
+        scratch_shapes=[pltpu.SemaphoreType.DMA((2,))],
+    )(moved, swept)
+
+
+def deliver(moved_ref, swept_ref, out_ref, solid_ref, sem):
+    copies = [
+        pltpu.make_async_copy(moved_ref, out_ref, sem.at[0]),
+        pltpu.make_async_copy(swept_ref, solid_ref, sem.at[1]),
+    ]
+    for copy in copies:
+        copy.start()
+    for copy in copies:
+        copy.wait()
 
 
 def solution(mesh):

time: 26.2 us -> 22.9 us (0.87)
  local copies, waits for them, and re-layouts: 7.52 us -> 1.69 us
  Pallas kernels: 17.7 us -> 20.4 us
    unnamed x16 -> x4, local copies, waits for them, and re-layouts: 7.52 us -> 1.69 us
    pallas_call x1 -> x2, Pallas kernels: 17.7 us -> 20.4 us  [the longest x1 18 us: body(): pl.pallas_call(functools.partial(kernel, sizes), out_shape=(pltpu.VMEM(po...]
where the time goes in v2:
time: 22.9 us; the launch traced here: 22.7 us
  Pallas kernels  20.4 us (89%)
  local copies, waits for them, and re-layouts  1.69 us (7%)
  between operations  0.65 us (3%)
    pallas_call x1, Pallas kernels, body(): pl.pallas_call(functools.partial(kernel, sizes), out_shape=(pltpu.VMEM(po...  18 us
    pallas_call x1, Pallas kernels, body(): pl.pallas_call(deliver, out_shape=(pltpu.HBM(populations.shape, jnp.float...  2.38 us
    unnamed x4, local copies, waits for them, and re-layouts  1.69 us

profile of v2, /device:TPU:0, one launch (start us, length us, event | category | flops | bytes accessed | tf_op | source)
XLA Modules:
  0.0 22.7 jit_solution(6992272604699537590)
XLA Ops:
  0.6 18.0 %shard_map.86 = (f32[19,4,16,256]{3,2,1,0:T(8,128)S(1)}, f32[4,64,128]{2,1,0:T(8,128)S(1)}) custom-call(f32[19,4,16,256]{3,2,1,0:T(8,128)} %pops_ref.1, f32[4,64,128]{2,1,0:T(8,128)} %temp_ref.1, f32[4,64,128]{2,1,0:T(8,128)} %diff_ref.1, s32[4,256]{1,0:T(4,128)} %nozzle_hbm.1, s32[4,256]{1,0:T(4,128)} %wall_hbm.1, f32[4,128]{1,0:T(4,128)} %load_hbm.1, ...), custom_call_target="tpu_custom_call" | custom-call | tf_op jit(solution)/shard_map/pallas_call | solution.py:406
  18.7 0.0 copy-start
  18.7 1.0 %copy-done = f32[19,4,16,256]{3,2,1,0:T(8,128)} copy-done((f32[19,4,16,256]{3,2,1,0:T(8,128)}, f32[19,4,16,256]{3,2,1,0:T(8,128)S(1)}, u32[]{:S(2)}) %copy-start) | copy-done | bytes 1245208
  19.7 0.0 copy-start.1
  19.7 0.6 %copy-done.1 = f32[4,64,128]{2,1,0:T(8,128)} copy-done((f32[4,64,128]{2,1,0:T(8,128)}, f32[4,64,128]{2,1,0:T(8,128)S(1)}, u32[]{:S(2)}) %copy-start.1) | copy-done | bytes 131096
  20.4 2.4 %shard_map.87 = (f32[19,4,16,256]{3,2,1,0:T(8,128)}, f32[4,64,128]{2,1,0:T(8,128)}) custom-call(f32[19,4,16,256]{3,2,1,0:T(8,128)} %copy-done, f32[4,64,128]{2,1,0:T(8,128)} %copy-done.1), custom_call_target="tpu_custom_call" | custom-call | tf_op jit(solution)/shard_map/pallas_call | solution.py:423
Async XLA Ops:
  18.7 1.0 %copy-start = (f32[19,4,16,256]{3,2,1,0:T(8,128)}, f32[19,4,16,256]{3,2,1,0:T(8,128)S(1)}, u32[]{:S(2)}) copy-start(f32[19,4,16,256]{3,2,1,0:T(8,128)S(1)} %get-tuple-element.4.moved_ref) | copy-start | bytes 3735556
  19.7 0.7 %copy-start.1 = (f32[4,64,128]{2,1,0:T(8,128)}, f32[4,64,128]{2,1,0:T(8,128)S(1)}, u32[]{:S(2)}) copy-start(f32[4,64,128]{2,1,0:T(8,128)S(1)} %get-tuple-element.5.swept_ref) | copy-start | bytes 393220

commit v3 on v2

--- a/solution.py
+++ b/solution.py
@@ -184,7 +184,7 @@
         return carry
 
     lax.fori_loop(0, 2, collide_plane, 0)
-    face_in, edge_in = [], []
+    face_in, corner_in, edge_in = [], [], []
     for side, (edge, dx) in enumerate(((X - 1, 1), (0, -1))):
         face_in.append(
             send(post.at[pl.ds(side * FACE, FACE), edge], px_in.at[side], device(dx, 0, 0))
@@ -192,7 +192,7 @@
     for side, (edge, dx) in enumerate(((X - 1, 1), (0, -1))):
         for flank, (lane, dy) in enumerate(((Y - LANES, 1), (0, -1))):
             member = SLOT[INDEX[(dx, dy, 0)]]
-            edge_in.append(send(
+            corner_in.append(send(
                 post.at[member, edge, :, pl.ds(lane, LANES)], xy_in.at[side, flank],
                 device(dx, dy, 0),
             ))
@@ -202,9 +202,9 @@
         copy.wait()
     halved = [0.5 * tile for tile in blocks(diff)]
     sy_out[0] = edge_pack(blocks(temp) + halved, True)
-    sink_in.append(send(sy_out.at[0], sy_in.at[0], ahead))
+    flank_in = [send(sy_out.at[0], sy_in.at[0], ahead)]
     sy_out[1] = edge_pack(blocks(temp) + halved, False)
-    sink_in.append(send(sy_out.at[1], sy_in.at[1], behind))
+    flank_in.append(send(sy_out.at[1], sy_in.at[1], behind))
 
     for x in range(X):
         heat_out[x:x + 1, :] = heat[x, 0:1, W:2 * W]
@@ -233,7 +233,7 @@
                 yz_out[1, x:x + 1, :] = row[:, :LANES]
     edge_in.append(send(pz_out, pz_in, device(0, 0, 1)))
     for side, s in enumerate((1, -1)):
-        edge_in.append(send(xz_out.at[side], xz_in.at[side], device(s, 0, 1)))
+        corner_in.append(send(xz_out.at[side], xz_in.at[side], device(s, 0, 1)))
         edge_in.append(send(yz_out.at[side], yz_in.at[side], device(0, s, 1)))
 
     lane = lanes_like((D, W))
@@ -249,18 +249,12 @@
         )
         return low, high
 
-    for copy in sink_in:
-        copy.wait_recv()
-    heat_copy.wait_recv()
-    for copy in planes:
-        copy.wait()
-    packs = (sy_in[0], sy_in[1])
-    for x in range(X):
+    def sweep_first(x):
         own, cond = temp[x], 0.5 * diff[x]
         below = (temp[x - 1], diff[x - 1]) if x > 0 else (sx_in[0, 0], sx_in[0, 1])
         above = (temp[x + 1], diff[x + 1]) if x < X - 1 else (sx_in[1, 0], sx_in[1, 1])
-        temps = [below[0], above[0], *beside(own, packs, x, 0)]
-        conds = [0.5 * below[1], 0.5 * above[1], *beside(cond, packs, x, column)]
+        temps = [below[0], above[0], *beside(own, (sy_in[0], sy_in[1]), x, 0)]
+        conds = [0.5 * below[1], 0.5 * above[1], *beside(cond, (sy_in[0], sy_in[1]), x, column)]
         g = [cond + c for c in conds]
         g.append(jnp.where(depth == D - 1, 0.0, cond + turned(cond, -1, 0)))
         g.append(jnp.where(depth == 0, 0.0, cond + turned(cond, 1, 0)))
@@ -278,14 +272,6 @@
         base[x] = start
         inverse[x] = flip
         first[x] = numer * flip
-    first_in = []
-    for side, (edge, dx) in enumerate(((X - 1, 1), (0, -1))):
-        first_in.append(send(first.at[edge], fx_in.at[side], device(dx, 0, 0)))
-    fy_out[0] = edge_pack(blocks(first), True)
-    first_in.append(send(fy_out.at[0], fy_in.at[0], ahead))
-    fy_out[1] = edge_pack(blocks(first), False)
-    first_in.append(send(fy_out.at[1], fy_in.at[1], behind))
-
     wide = lanes_like((Z, Y))
     flat = lanes_like((1, Y))
     level = rows_like((Z, Y))
@@ -296,10 +282,7 @@
         spot = 0 if b == 1 else Y - 1
         return jnp.where(lanes == spot, edge, turned(value, b, 1))
 
-    for copy in edge_in:
-        copy.wait_recv()
     tall = Z // ROWS
-    py_packs = (py_in[0], py_in[1])
 
     def assemble(x):
         height_rows = {}
@@ -326,7 +309,7 @@
                 if inside:
                     begin = (ACROSS.index((a, c)) * X + source) * tall
                     border = edge_column(
-                        py_packs[flank], range(begin, begin + tall), b == -1
+                        py_in[flank], range(begin, begin + tall), b == -1
                     )
                 else:
                     border = turned(xy_in[side, flank], b, 1)
@@ -347,25 +330,50 @@
                     value = jnp.where(level == Z - 1, row, value)
             out_ref[i, x] = value
 
-    for x in range(1, X - 1):
-        assemble(x)
-    for copy in face_in:
-        copy.wait_recv()
-    assemble(0)
-    assemble(X - 1)
-
-    for copy in first_in:
-        copy.wait_recv()
-    packs = (fy_in[0], fy_in[1])
-    for x in range(X):
+    def sweep_second(x):
         own = first[x]
         below = first[x - 1] if x > 0 else fx_in[0]
         above = first[x + 1] if x < X - 1 else fx_in[1]
-        temps = [below, above, *beside(own, packs, x, 0), turned(own, -1, 0), turned(own, 1, 0)]
+        sides = beside(own, (fy_in[0], fy_in[1]), x, 0)
+        temps = [below, above, *sides, turned(own, -1, 0), turned(own, 1, 0)]
         numer = base[x]
         for k in range(6):
             numer = numer + links[k, x] * temps[k]
         solid_ref[x] = numer * inverse[x]
+
+    inner = range(1, X - 1)
+    for copy in edge_in:
+        copy.wait_recv()
+    for copy in planes:
+        copy.wait()
+    for x in inner:
+        assemble(x)
+    for copy in flank_in + [heat_copy]:
+        copy.wait_recv()
+    for x in inner:
+        sweep_first(x)
+    for copy in sink_in:
+        copy.wait_recv()
+    first_in = []
+    for side, (edge, dx) in enumerate(((X - 1, 1), (0, -1))):
+        sweep_first(edge)
+        first_in.append(send(first.at[edge], fx_in.at[side], device(dx, 0, 0)))
+    fy_out[0] = edge_pack(blocks(first), True)
+    beside_in = [send(fy_out.at[0], fy_in.at[0], ahead)]
+    fy_out[1] = edge_pack(blocks(first), False)
+    beside_in.append(send(fy_out.at[1], fy_in.at[1], behind))
+    for copy in corner_in + face_in:
+        copy.wait_recv()
+    assemble(0)
+    assemble(X - 1)
+    for copy in beside_in:
+        copy.wait_recv()
+    for x in inner:
+        sweep_second(x)
+    for copy in first_in:
+        copy.wait_recv()
+    sweep_second(0)
+    sweep_second(X - 1)
     for copy in sent:
         copy.wait_send()
 
@@ -426,10 +434,11 @@
             pltpu.HBM(populations.shape, jnp.float32),
             pltpu.HBM(solid_temp.shape, jnp.float32),
         ),
-        in_specs=[local, local],
+        in_specs=[pl.BlockSpec(memory_space=pl.ANY)] * 2,
         out_specs=[far, far],
         scratch_shapes=[pltpu.SemaphoreType.DMA((2,))],
-    )(moved, swept)
+        compiler_params=pltpu.CompilerParams(vmem_limit_bytes=1024 * 1024),
+    )(*(pltpu.with_memory_space_constraint(value, pltpu.VMEM) for value in (moved, swept)))
 
 
 def deliver(moved_ref, swept_ref, out_ref, solid_ref, sem):

time: 22.9 us -> 19.6 us (0.86)
  local copies, waits for them, and re-layouts: 1.69 us -> 0 us
  Pallas kernels: 20.4 us -> 18.8 us
    unnamed x4 -> x0, local copies, waits for them, and re-layouts: 1.69 us -> none
    pallas_call x1, Pallas kernels: 2.38 us -> 1.08 us  [body(): pl.pallas_call(deliver, out_shape=(pltpu.HBM(populations.shape, jnp.float...]
    pallas_call x1, Pallas kernels: 18 us -> 17.7 us  [body(): pl.pallas_call(functools.partial(kernel, sizes), out_shape=(pltpu.VMEM(po...]
where the time goes in v3:
time: 19.6 us; the launch traced here: 19.5 us
  Pallas kernels  18.8 us (96%)
  between operations  0.64 us (3%)
    pallas_call x1, Pallas kernels, body(): pl.pallas_call(functools.partial(kernel, sizes), out_shape=(pltpu.VMEM(po...  17.7 us
    pallas_call x1, Pallas kernels, body(): pl.pallas_call(deliver, out_shape=(pltpu.HBM(populations.shape, jnp.float...  1.08 us

profile of v3, /device:TPU:0, one launch (start us, length us, event | category | flops | bytes accessed | tf_op | source)
XLA Modules:
  0.0 19.5 jit_solution(12484511296307117345)
XLA Ops:
  0.6 17.7 %shard_map.86 = (f32[19,4,16,256]{3,2,1,0:T(8,128)S(1)}, f32[4,64,128]{2,1,0:T(8,128)S(1)}) custom-call(f32[19,4,16,256]{3,2,1,0:T(8,128)} %pops_ref.1, f32[4,64,128]{2,1,0:T(8,128)} %temp_ref.1, f32[4,64,128]{2,1,0:T(8,128)} %diff_ref.1, s32[4,256]{1,0:T(4,128)} %nozzle_hbm.1, s32[4,256]{1,0:T(4,128)} %wall_hbm.1, f32[4,128]{1,0:T(4,128)} %load_hbm.1, ...), custom_call_target="tpu_custom_call" | custom-call | tf_op jit(solution)/shard_map/pallas_call | solution.py:414
  18.4 1.1 %shard_map.87 = (f32[19,4,16,256]{3,2,1,0:T(8,128)}, f32[4,64,128]{2,1,0:T(8,128)}) custom-call(f32[19,4,16,256]{3,2,1,0:T(8,128)S(1)} %get-tuple-element.4.moved_ref, f32[4,64,128]{2,1,0:T(8,128)S(1)} %get-tuple-element.5.swept_ref), custom_call_target="tpu_custom_call" | custom-call | tf_op jit(solution)/shard_map/pallas_call | solution.py:431

commit v4 on v3

--- a/solution.py
+++ b/solution.py
@@ -102,8 +102,8 @@
 
 def kernel(sizes, pops_ref, temp_ref, diff_ref, nozzle_hbm, wall_hbm, load_hbm, cool_hbm,
            out_ref, solid_ref, nozzle_ref, wall_ref, load_ref, cool_ref, pops, post, temp, diff, first, links, base, inverse, heat,
-           sx_in, sy_out, sy_in, heat_out, heat_in, px_in, py_out, py_in, pz_out, pz_in,
-           xy_in, xz_out, xz_in, yz_out, yz_in, fx_in, fy_out, fy_in,
+           sx_in, sy_out, sy_in, heat_out, heat_in, px_out, px_in, py_out, py_in, pz_out, pz_in,
+           yz_out, yz_in, fx_in, fy_out, fy_in,
            load_sem, send_sem, recv_sem):
     nx, ny, nz = sizes
     gx, gy, gz = (lax.axis_index(name) for name in ("gx", "gy", "gz"))
@@ -120,8 +120,7 @@
     near = set()
     for dx, dy, other in (
         [(s, 0, 0) for s in (1, -1)] + [(0, s, 0) for s in (1, -1)] + [(0, 0, 1)]
-        + [(s, t, 0) for s in (1, -1) for t in (1, -1)]
-        + [(s, 0, 1) for s in (1, -1)] + [(0, s, 1) for s in (1, -1)]
+        + [(0, s, 1) for s in (1, -1)]
     ):
         near.add((dx % nx, dy % ny, other))
     barrier = pltpu.get_barrier_semaphore()
@@ -183,32 +182,8 @@
                     heat[x, :, y:y + LANES] = H_BASE + H_GAIN * square
         return carry
 
-    lax.fori_loop(0, 2, collide_plane, 0)
-    face_in, corner_in, edge_in = [], [], []
-    for side, (edge, dx) in enumerate(((X - 1, 1), (0, -1))):
-        face_in.append(
-            send(post.at[pl.ds(side * FACE, FACE), edge], px_in.at[side], device(dx, 0, 0))
-        )
-    for side, (edge, dx) in enumerate(((X - 1, 1), (0, -1))):
-        for flank, (lane, dy) in enumerate(((Y - LANES, 1), (0, -1))):
-            member = SLOT[INDEX[(dx, dy, 0)]]
-            corner_in.append(send(
-                post.at[member, edge, :, pl.ds(lane, LANES)], xy_in.at[side, flank],
-                device(dx, dy, 0),
-            ))
-    lax.fori_loop(2, X, collide_plane, 0)
-
-    for copy in loads:
-        copy.wait()
-    halved = [0.5 * tile for tile in blocks(diff)]
-    sy_out[0] = edge_pack(blocks(temp) + halved, True)
-    flank_in = [send(sy_out.at[0], sy_in.at[0], ahead)]
-    sy_out[1] = edge_pack(blocks(temp) + halved, False)
-    flank_in.append(send(sy_out.at[1], sy_in.at[1], behind))
-
-    for x in range(X):
-        heat_out[x:x + 1, :] = heat[x, 0:1, W:2 * W]
-    heat_copy = send(heat_out, heat_in, device(0, 0, 1))
+    lax.fori_loop(0, X, collide_plane, 0)
+    face_in, edge_in = [], []
 
     for side, (lane, dy) in enumerate(((Y - LANES, 1), (0, -1))):
         tiles = [
@@ -225,16 +200,25 @@
                 post[SLOT[INDEX[(a, b, -1)]], x, 0:1, :],
             )
             pz_out[k * X + x:k * X + x + 1, :] = row
-            if (a, x) in ((1, X - 1), (-1, 0)):
-                xz_out[0 if a == 1 else 1, 0:1, :] = row
             if b == 1:
                 yz_out[0, x:x + 1, :] = row[:, Y - LANES:]
             if b == -1:
                 yz_out[1, x:x + 1, :] = row[:, :LANES]
     edge_in.append(send(pz_out, pz_in, device(0, 0, 1)))
     for side, s in enumerate((1, -1)):
-        corner_in.append(send(xz_out.at[side], xz_in.at[side], device(s, 0, 1)))
         edge_in.append(send(yz_out.at[side], yz_in.at[side], device(0, s, 1)))
+
+    for x in range(X):
+        heat_out[x:x + 1, :] = heat[x, 0:1, W:2 * W]
+    heat_copy = send(heat_out, heat_in, device(0, 0, 1))
+
+    for copy in loads:
+        copy.wait()
+    halved = [0.5 * tile for tile in blocks(diff)]
+    sy_out[0] = edge_pack(blocks(temp) + halved, True)
+    flank_in = [send(sy_out.at[0], sy_in.at[0], ahead)]
+    sy_out[1] = edge_pack(blocks(temp) + halved, False)
+    flank_in.append(send(sy_out.at[1], sy_in.at[1], behind))
 
     lane = lanes_like((D, W))
     depth = rows_like((D, W))
@@ -284,50 +268,45 @@
 
     tall = Z // ROWS
 
-    def assemble(x):
-        height_rows = {}
-        for k, (a, b) in enumerate(ACROSS):
-            source = x - a
-            if 0 <= source < X:
-                row = pz_in[k * X + source:k * X + source + 1, :]
-            else:
-                row = xz_in[0 if a == 1 else 1, 0:1, :]
+    floor = level == jnp.where(lowest, 0, -1)
+    roof = level == jnp.where(lowest, -1, Z - 1)
+
+    def move(i, source):
+        a, b, c = VELOCITIES[i]
+        value = post[SLOT[i], source]
+        if b != 0:
+            flank = 0 if b == 1 else 1
+            begin = (ACROSS.index((a, c)) * X + source) * tall
+            border = edge_column(py_in[flank], range(begin, begin + tall), b == -1)
+            value = shifted(value, wide, border, b)
+        if c != 0:
+            at = ACROSS.index((a, b)) * X + source
+            row = pz_in[at:at + 1, :]
             if b != 0:
-                flank = 0 if b == 1 else 1
-                border = turned(yz_in[flank], b, 1)[x:x + 1, :]
-                row = shifted(row, flat, border, b)
-            height_rows[(a, b)] = row
+                row = shifted(row, flat, turned(yz_in[flank], b, 1)[source:source + 1, :], b)
+            value = jnp.where(level == (0 if c == 1 else Z - 1), row, turned(value, c, 0))
+        return value
+
+    def assemble(x, members):
         nozzle = nozzle_ref[x:x + 1, :] == 1
         outlet = wall_ref[x:x + 1, :] == 1
-        for i, (a, b, c) in enumerate(VELOCITIES):
-            source = x - a
-            side = 0 if a == 1 else 1
-            inside = 0 <= source < X
-            value = post[SLOT[i], source] if inside else px_in[side, SLOT[i] - side * FACE]
-            if b != 0:
-                flank = 0 if b == 1 else 1
-                if inside:
-                    begin = (ACROSS.index((a, c)) * X + source) * tall
-                    border = edge_column(
-                        py_in[flank], range(begin, begin + tall), b == -1
-                    )
-                else:
-                    border = turned(xy_in[side, flank], b, 1)
-                value = shifted(value, wide, border, b)
-            if c != 0:
-                value = turned(value, c, 0)
-                back = SLOT[OPPOSITE[i]]
-                if c == 1:
-                    row = jnp.where(lowest, post[back, x, 0:1, :], height_rows[(a, b)])
-                    value = jnp.where(level == 0, row, value)
-                else:
-                    closed = post[back, x, Z - 1:Z, :]
-                    jet = closed + 6.0 * WEIGHTS[i] * JET_SPEED
-                    plate = jnp.where(
-                        nozzle, jet, jnp.where(outlet, post[SLOT[i], x, Z - 1:Z, :], closed)
-                    )
-                    row = jnp.where(lowest, height_rows[(a, b)], plate)
-                    value = jnp.where(level == Z - 1, row, value)
+        for i in members:
+            a, b, c = VELOCITIES[i]
+            if 0 <= x - a < X:
+                value = move(i, x - a)
+            else:
+                side = 0 if a == 1 else 1
+                value = px_in[side, SLOT[i] - side * FACE]
+            back = SLOT[OPPOSITE[i]]
+            if c == 1:
+                value = jnp.where(floor, post[back, x, 0:1, :], value)
+            if c == -1:
+                closed = post[back, x, Z - 1:Z, :]
+                jet = closed + 6.0 * WEIGHTS[i] * JET_SPEED
+                plate = jnp.where(
+                    nozzle, jet, jnp.where(outlet, post[SLOT[i], x, Z - 1:Z, :], closed)
+                )
+                value = jnp.where(roof, plate, value)
             out_ref[i, x] = value
 
     def sweep_second(x):
@@ -342,12 +321,15 @@
         solid_ref[x] = numer * inverse[x]
 
     inner = range(1, X - 1)
+    own = {x: [i for i in range(COUNT) if 0 <= x - VELOCITIES[i][0] < X] for x in range(X)}
     for copy in edge_in:
         copy.wait_recv()
+    for side, (edge, dx) in enumerate(((X - 1, 1), (0, -1))):
+        for k in range(FACE):
+            px_out[side, k] = move(ORDER[side * FACE + k], edge)
+        face_in.append(send(px_out.at[side], px_in.at[side], device(dx, 0, 0)))
     for copy in planes:
         copy.wait()
-    for x in inner:
-        assemble(x)
     for copy in flank_in + [heat_copy]:
         copy.wait_recv()
     for x in inner:
@@ -362,10 +344,8 @@
     beside_in = [send(fy_out.at[0], fy_in.at[0], ahead)]
     fy_out[1] = edge_pack(blocks(first), False)
     beside_in.append(send(fy_out.at[1], fy_in.at[1], behind))
-    for copy in corner_in + face_in:
-        copy.wait_recv()
-    assemble(0)
-    assemble(X - 1)
+    for x in range(X):
+        assemble(x, own[x])
     for copy in beside_in:
         copy.wait_recv()
     for x in inner:
@@ -374,6 +354,10 @@
         copy.wait_recv()
     sweep_second(0)
     sweep_second(X - 1)
+    for copy in face_in:
+        copy.wait_recv()
+    for x in (0, X - 1):
+        assemble(x, [i for i in range(COUNT) if i not in own[x]])
     for copy in sent:
         copy.wait_send()
 
@@ -400,14 +384,13 @@
         vmem(X, ROWS, Y),
         vmem(2, 2, D, W), pair, pair,
         vmem(tall, W), vmem(tall, W),
-        vmem(2, FACE, Z, Y), pair, pair,
+        vmem(2, FACE, Z, Y), vmem(2, FACE, Z, Y), pair, pair,
         vmem(rows, Y), vmem(rows, Y),
-        vmem(2, 2, Z, LANES), vmem(2, ROWS, Y), vmem(2, ROWS, Y),
         vmem(2, tall, LANES), vmem(2, tall, LANES),
         vmem(2, D, W), pair, pair,
         pltpu.SemaphoreType.DMA((X + 6,)),
-        pltpu.SemaphoreType.DMA((24,)),
-        pltpu.SemaphoreType.DMA((24,)),
+        pltpu.SemaphoreType.DMA((18,)),
+        pltpu.SemaphoreType.DMA((18,)),
     ]
     far = pl.BlockSpec(memory_space=pltpu.HBM)
     local = pl.BlockSpec(memory_space=pltpu.VMEM)

time: 19.6 us -> 17.7 us (0.903)
  Pallas kernels: 18.8 us -> 16.9 us
    pallas_call x1, Pallas kernels: 17.7 us -> 15.9 us  [body(): pl.pallas_call(functools.partial(kernel, sizes), out_shape=(pltpu.VMEM(po...]
where the time goes in v4:
time: 17.7 us; the launch traced here: 17.6 us
  Pallas kernels  16.9 us (95%)
  between operations  0.64 us (4%)
    pallas_call x1, Pallas kernels, body(): pl.pallas_call(functools.partial(kernel, sizes), out_shape=(pltpu.VMEM(po...  15.9 us
    pallas_call x1, Pallas kernels, body(): pl.pallas_call(deliver, out_shape=(pltpu.HBM(populations.shape, jnp.float...  1.08 us

profile of v4, /device:TPU:0, one launch (start us, length us, event | category | flops | bytes accessed | tf_op | source)
XLA Modules:
  0.0 17.6 jit_solution(2864231011670129486)
XLA Ops:
  0.6 15.9 %shard_map.86 = (f32[19,4,16,256]{3,2,1,0:T(8,128)S(1)}, f32[4,64,128]{2,1,0:T(8,128)S(1)}) custom-call(f32[19,4,16,256]{3,2,1,0:T(8,128)} %pops_ref.1, f32[4,64,128]{2,1,0:T(8,128)} %temp_ref.1, f32[4,64,128]{2,1,0:T(8,128)} %diff_ref.1, s32[4,256]{1,0:T(4,128)} %nozzle_hbm.1, s32[4,256]{1,0:T(4,128)} %wall_hbm.1, f32[4,128]{1,0:T(4,128)} %load_hbm.1, ...), custom_call_target="tpu_custom_call" | custom-call | tf_op jit(solution)/shard_map/pallas_call | solution.py:397
  16.5 1.1 %shard_map.87 = (f32[19,4,16,256]{3,2,1,0:T(8,128)}, f32[4,64,128]{2,1,0:T(8,128)}) custom-call(f32[19,4,16,256]{3,2,1,0:T(8,128)S(1)} %get-tuple-element.4.moved_ref, f32[4,64,128]{2,1,0:T(8,128)S(1)} %get-tuple-element.5.swept_ref), custom_call_target="tpu_custom_call" | custom-call | tf_op jit(solution)/shard_map/pallas_call | solution.py:414

commit v5 on v4

--- a/solution.py
+++ b/solution.py
@@ -82,8 +82,11 @@
 
 
 def turned(value, shift, axis):
-    shift = shift % value.shape[axis]
-    return value if shift == 0 else pltpu.roll(value, shift, axis)
+    size = value.shape[axis]
+    if isinstance(shift, int):
+        shift = shift % size
+        return value if shift == 0 else pltpu.roll(value, shift, axis)
+    return pltpu.roll(value, lax.rem(shift + size, size), axis)
 
 
 def edge_pack(tiles, last):
@@ -102,8 +105,8 @@
 
 def kernel(sizes, pops_ref, temp_ref, diff_ref, nozzle_hbm, wall_hbm, load_hbm, cool_hbm,
            out_ref, solid_ref, nozzle_ref, wall_ref, load_ref, cool_ref, pops, post, temp, diff, first, links, base, inverse, heat,
-           sx_in, sy_out, sy_in, heat_out, heat_in, px_out, px_in, py_out, py_in, pz_out, pz_in,
-           yz_out, yz_in, fx_in, fy_out, fy_in,
+           sy_out, sy_in, heat_out, heat_in, px_out, px_in, py_out, py_in, pz_out, pz_in,
+           yz_out, yz_in, fy_out, fy_in,
            load_sem, send_sem, recv_sem):
     nx, ny, nz = sizes
     gx, gy, gz = (lax.axis_index(name) for name in ("gx", "gy", "gz"))
@@ -130,8 +133,8 @@
         )
 
     loads = [
-        pltpu.make_async_copy(temp_ref, temp, load_sem.at[X]),
-        pltpu.make_async_copy(diff_ref, diff, load_sem.at[X + 1]),
+        pltpu.make_async_copy(temp_ref, temp.at[pl.ds(1, X)], load_sem.at[X]),
+        pltpu.make_async_copy(diff_ref, diff.at[pl.ds(1, X)], load_sem.at[X + 1]),
     ]
     planes = [
         pltpu.make_async_copy(far, near_by, load_sem.at[X + 2 + k])
@@ -161,13 +164,13 @@
         return copy
 
     def blocks(ref):
-        return [ref[x, z:z + ROWS, :] for x in range(X) for z in range(0, D, ROWS)]
+        return [ref[1 + x, z:z + ROWS, :] for x in range(X) for z in range(0, D, ROWS)]
 
     pl.semaphore_wait(barrier, len(near))
     sink_in = []
-    for side, (edge, dx) in enumerate(((X - 1, 1), (0, -1))):
-        sink_in.append(send(temp_ref.at[edge], sx_in.at[side, 0], device(dx, 0, 0)))
-        sink_in.append(send(diff_ref.at[edge], sx_in.at[side, 1], device(dx, 0, 0)))
+    for edge, slot, dx in ((X - 1, 0, 1), (0, X + 1, -1)):
+        sink_in.append(send(temp_ref.at[edge], temp.at[slot], device(dx, 0, 0)))
+        sink_in.append(send(diff_ref.at[edge], diff.at[slot], device(dx, 0, 0)))
 
     def collide_plane(step, carry):
         x = lax.rem(step + X - 1, X)
@@ -226,26 +229,25 @@
     column = depth_blocks * X
 
     def beside(value, packs, x, start):
-        places = range(start + x * depth_blocks, start + (x + 1) * depth_blocks)
+        places = [start + x * depth_blocks + k for k in range(depth_blocks)]
         low = jnp.where(lane == 0, edge_column(packs[0], places, False), turned(value, 1, 1))
         high = jnp.where(
             lane == W - 1, edge_column(packs[1], places, True), turned(value, -1, 1)
         )
         return low, high
 
-    def sweep_first(x):
-        own, cond = temp[x], 0.5 * diff[x]
-        below = (temp[x - 1], diff[x - 1]) if x > 0 else (sx_in[0, 0], sx_in[0, 1])
-        above = (temp[x + 1], diff[x + 1]) if x < X - 1 else (sx_in[1, 0], sx_in[1, 1])
+    def sweep_first(x, carry):
+        own, cond = temp[x + 1], 0.5 * diff[x + 1]
+        below, above = (temp[x], diff[x]), (temp[x + 2], diff[x + 2])
         temps = [below[0], above[0], *beside(own, (sy_in[0], sy_in[1]), x, 0)]
         conds = [0.5 * below[1], 0.5 * above[1], *beside(cond, (sy_in[0], sy_in[1]), x, column)]
         g = [cond + c for c in conds]
         g.append(jnp.where(depth == D - 1, 0.0, cond + turned(cond, -1, 0)))
         g.append(jnp.where(depth == 0, 0.0, cond + turned(cond, 1, 0)))
         temps += [turned(own, -1, 0), turned(own, 1, 0)]
-        warm = jnp.where(lowest, heat[x, 0:1, 0:W], heat_in[x:x + 1, :])
-        start = own + jnp.where(depth == 0, load_ref[x:x + 1, :], 0.0)
-        start = start + jnp.where(depth == D - 1, warm * cool_ref[x:x + 1, :], 0.0)
+        warm = jnp.where(lowest, heat[x, 0:1, 0:W], heat_in[pl.ds(x, 1), :])
+        start = own + jnp.where(depth == 0, load_ref[pl.ds(x, 1), :], 0.0)
+        start = start + jnp.where(depth == D - 1, warm * cool_ref[pl.ds(x, 1), :], 0.0)
         denom = 1.0 + jnp.where(depth == D - 1, warm, 0.0)
         numer = start
         for k in range(6):
@@ -255,7 +257,9 @@
         flip = 1.0 / denom
         base[x] = start
         inverse[x] = flip
-        first[x] = numer * flip
+        first[x + 1] = numer * flip
+        return carry
+
     wide = lanes_like((Z, Y))
     flat = lanes_like((1, Y))
     level = rows_like((Z, Y))
@@ -277,51 +281,47 @@
         if b != 0:
             flank = 0 if b == 1 else 1
             begin = (ACROSS.index((a, c)) * X + source) * tall
-            border = edge_column(py_in[flank], range(begin, begin + tall), b == -1)
+            places = [begin + k for k in range(tall)]
+            border = edge_column(py_in[flank], places, b == -1)
             value = shifted(value, wide, border, b)
         if c != 0:
-            at = ACROSS.index((a, b)) * X + source
-            row = pz_in[at:at + 1, :]
+            row = pz_in[pl.ds(ACROSS.index((a, b)) * X + source, 1), :]
             if b != 0:
-                row = shifted(row, flat, turned(yz_in[flank], b, 1)[source:source + 1, :], b)
+                row = shifted(row, flat, turned(yz_in[flank, pl.ds(source, 1), :], b, 1), b)
             value = jnp.where(level == (0 if c == 1 else Z - 1), row, turned(value, c, 0))
         return value
 
-    def assemble(x, members):
-        nozzle = nozzle_ref[x:x + 1, :] == 1
-        outlet = wall_ref[x:x + 1, :] == 1
-        for i in members:
-            a, b, c = VELOCITIES[i]
-            if 0 <= x - a < X:
-                value = move(i, x - a)
-            else:
-                side = 0 if a == 1 else 1
-                value = px_in[side, SLOT[i] - side * FACE]
-            back = SLOT[OPPOSITE[i]]
-            if c == 1:
-                value = jnp.where(floor, post[back, x, 0:1, :], value)
-            if c == -1:
-                closed = post[back, x, Z - 1:Z, :]
-                jet = closed + 6.0 * WEIGHTS[i] * JET_SPEED
-                plate = jnp.where(
-                    nozzle, jet, jnp.where(outlet, post[SLOT[i], x, Z - 1:Z, :], closed)
-                )
-                value = jnp.where(roof, plate, value)
-            out_ref[i, x] = value
-
-    def sweep_second(x):
-        own = first[x]
-        below = first[x - 1] if x > 0 else fx_in[0]
-        above = first[x + 1] if x < X - 1 else fx_in[1]
+    def assemble(x, carry):
+        for i, (a, _, _) in enumerate(VELOCITIES):
+            source = x if a == 0 else jnp.clip(x - a, 0, X - 1)
+            settle(i, x, move(i, source))
+        return carry
+
+    def settle(i, x, value):
+        c = VELOCITIES[i][2]
+        back = SLOT[OPPOSITE[i]]
+        if c == 1:
+            value = jnp.where(floor, post[back, x, 0:1, :], value)
+        if c == -1:
+            closed = post[back, x, Z - 1:Z, :]
+            jet = closed + 6.0 * WEIGHTS[i] * JET_SPEED
+            open_value = post[SLOT[i], x, Z - 1:Z, :]
+            nozzle = nozzle_ref[pl.ds(x, 1), :] == 1
+            outlet = wall_ref[pl.ds(x, 1), :] == 1
+            plate = jnp.where(nozzle, jet, jnp.where(outlet, open_value, closed))
+            value = jnp.where(roof, plate, value)
+        out_ref[i, x] = value
+
+    def sweep_second(x, carry):
+        own, below, above = first[x + 1], first[x], first[x + 2]
         sides = beside(own, (fy_in[0], fy_in[1]), x, 0)
         temps = [below, above, *sides, turned(own, -1, 0), turned(own, 1, 0)]
         numer = base[x]
         for k in range(6):
             numer = numer + links[k, x] * temps[k]
         solid_ref[x] = numer * inverse[x]
-
-    inner = range(1, X - 1)
-    own = {x: [i for i in range(COUNT) if 0 <= x - VELOCITIES[i][0] < X] for x in range(X)}
+        return carry
+
     for copy in edge_in:
         copy.wait_recv()
     for side, (edge, dx) in enumerate(((X - 1, 1), (0, -1))):
@@ -332,32 +332,28 @@
         copy.wait()
     for copy in flank_in + [heat_copy]:
         copy.wait_recv()
-    for x in inner:
-        sweep_first(x)
+    lax.fori_loop(1, X - 1, sweep_first, 0)
     for copy in sink_in:
         copy.wait_recv()
     first_in = []
-    for side, (edge, dx) in enumerate(((X - 1, 1), (0, -1))):
-        sweep_first(edge)
-        first_in.append(send(first.at[edge], fx_in.at[side], device(dx, 0, 0)))
+    lax.fori_loop(0, 2, lambda k, carry: sweep_first(k * (X - 1), carry), 0)
+    for edge, slot, dx in ((X, 0, 1), (1, X + 1, -1)):
+        first_in.append(send(first.at[edge], first.at[slot], device(dx, 0, 0)))
     fy_out[0] = edge_pack(blocks(first), True)
     beside_in = [send(fy_out.at[0], fy_in.at[0], ahead)]
     fy_out[1] = edge_pack(blocks(first), False)
     beside_in.append(send(fy_out.at[1], fy_in.at[1], behind))
-    for x in range(X):
-        assemble(x, own[x])
+    lax.fori_loop(0, X, assemble, 0)
     for copy in beside_in:
         copy.wait_recv()
-    for x in inner:
-        sweep_second(x)
     for copy in first_in:
         copy.wait_recv()
-    sweep_second(0)
-    sweep_second(X - 1)
+    lax.fori_loop(0, X, sweep_second, 0)
     for copy in face_in:
         copy.wait_recv()
-    for x in (0, X - 1):
-        assemble(x, [i for i in range(COUNT) if i not in own[x]])
+    for side, x in enumerate((0, X - 1)):
+        for k in range(FACE):
+            settle(ORDER[side * FACE + k], x, px_in[side, k])
     for copy in sent:
         copy.wait_send()
 
@@ -379,15 +375,15 @@
     scratch = [
         pltpu.VMEM((X, Y), jnp.int32), pltpu.VMEM((X, Y), jnp.int32), vmem(X, W), vmem(X, W),
         vmem(COUNT, X, Z, Y), vmem(COUNT, X, Z, Y),
-        vmem(X, D, W), vmem(X, D, W), vmem(X, D, W),
+        vmem(X + 2, D, W), vmem(X + 2, D, W), vmem(X + 2, D, W),
         vmem(6, X, D, W), vmem(X, D, W), vmem(X, D, W),
         vmem(X, ROWS, Y),
-        vmem(2, 2, D, W), pair, pair,
+        pair, pair,
         vmem(tall, W), vmem(tall, W),
         vmem(2, FACE, Z, Y), vmem(2, FACE, Z, Y), pair, pair,
         vmem(rows, Y), vmem(rows, Y),
         vmem(2, tall, LANES), vmem(2, tall, LANES),
-        vmem(2, D, W), pair, pair,
+        pair, pair,
         pltpu.SemaphoreType.DMA((X + 6,)),
         pltpu.SemaphoreType.DMA((18,)),
         pltpu.SemaphoreType.DMA((18,)),
@@ -419,16 +415,16 @@
         ),
         in_specs=[pl.BlockSpec(memory_space=pl.ANY)] * 2,
         out_specs=[far, far],
-        scratch_shapes=[pltpu.SemaphoreType.DMA((2,))],
+        scratch_shapes=[pltpu.SemaphoreType.DMA((populations.shape[1] + 1,))],
         compiler_params=pltpu.CompilerParams(vmem_limit_bytes=1024 * 1024),
     )(*(pltpu.with_memory_space_constraint(value, pltpu.VMEM) for value in (moved, swept)))
 
 
 def deliver(moved_ref, swept_ref, out_ref, solid_ref, sem):
-    copies = [
-        pltpu.make_async_copy(moved_ref, out_ref, sem.at[0]),
-        pltpu.make_async_copy(swept_ref, solid_ref, sem.at[1]),
-    ]
+    planes = moved_ref.shape[1]
+    copies = [pltpu.make_async_copy(swept_ref, solid_ref, sem.at[planes])]
+    for x in range(planes):
+        copies.append(pltpu.make_async_copy(moved_ref.at[:, x], out_ref.at[:, x], sem.at[x]))
     for copy in copies:
         copy.start()
     for copy in copies:

time: 17.7 us -> 18.3 us (1.034)
  Pallas kernels: 16.9 us -> 17.5 us
    pallas_call x1, Pallas kernels: 15.9 us -> 16.3 us  [body(): pl.pallas_call(functools.partial(kernel, sizes), out_shape=(pltpu.VMEM(po...]
where the time goes in v5:
time: 18.3 us; the launch traced here: 18.1 us
  Pallas kernels  17.5 us (96%)
  between operations  0.64 us (3%)
    pallas_call x1, Pallas kernels, body(): pl.pallas_call(functools.partial(kernel, sizes), out_shape=(pltpu.VMEM(po...  16.3 us
    pallas_call x1, Pallas kernels, body(): pl.pallas_call(deliver, out_shape=(pltpu.HBM(populations.shape, jnp.float...  1.11 us

profile of v5, /device:TPU:0, one launch (start us, length us, event | category | flops | bytes accessed | tf_op | source)
XLA Modules:
  0.0 18.1 jit_solution(5109791688655712783)
XLA Ops:
  0.6 16.3 %shard_map.86 = (f32[19,4,16,256]{3,2,1,0:T(8,128)S(1)}, f32[4,64,128]{2,1,0:T(8,128)S(1)}) custom-call(f32[19,4,16,256]{3,2,1,0:T(8,128)} %pops_ref.1, f32[4,64,128]{2,1,0:T(8,128)} %temp_ref.1, f32[4,64,128]{2,1,0:T(8,128)} %diff_ref.1, s32[4,256]{1,0:T(4,128)} %nozzle_hbm.1, s32[4,256]{1,0:T(4,128)} %wall_hbm.1, f32[4,128]{1,0:T(4,128)} %load_hbm.1, ...), custom_call_target="tpu_custom_call" | custom-call | tf_op jit(solution)/shard_map/pallas_call | solution.py:393
  17.0 1.1 %shard_map.87 = (f32[19,4,16,256]{3,2,1,0:T(8,128)}, f32[4,64,128]{2,1,0:T(8,128)}) custom-call(f32[19,4,16,256]{3,2,1,0:T(8,128)S(1)} %get-tuple-element.4.moved_ref, f32[4,64,128]{2,1,0:T(8,128)S(1)} %get-tuple-element.5.swept_ref), custom_call_target="tpu_custom_call" | custom-call | tf_op jit(solution)/shard_map/pallas_call | solution.py:410

commit v6 on v4

--- a/solution.py
+++ b/solution.py
@@ -182,8 +182,14 @@
                     heat[x, :, y:y + LANES] = H_BASE + H_GAIN * square
         return carry
 
-    lax.fori_loop(0, X, collide_plane, 0)
-    face_in, edge_in = [], []
+    face_in, edge_in, flank_edge_in = [], [], []
+    lax.fori_loop(0, 2, collide_plane, 0)
+    ends = ((X - 1, 1), (0, -1))
+    for side, (edge, dx) in enumerate(ends):
+        face_in.append(send(
+            post.at[SLOT[INDEX[(dx, 0, 0)]], edge], px_in.at[side, 0], device(dx, 0, 0)
+        ))
+    lax.fori_loop(2, X, collide_plane, 0)
 
     for side, (lane, dy) in enumerate(((Y - LANES, 1), (0, -1))):
         tiles = [
@@ -191,7 +197,7 @@
             for a, c in ACROSS for x in range(X) for z in range(0, Z, ROWS)
         ]
         py_out[side] = edge_pack(tiles, dy == 1)
-        edge_in.append(send(py_out.at[side], py_in.at[side], device(0, dy, 0)))
+        flank_edge_in.append(send(py_out.at[side], py_in.at[side], device(0, dy, 0)))
     for k, (a, b) in enumerate(ACROSS):
         for x in range(X):
             row = jnp.where(
@@ -211,14 +217,6 @@
     for x in range(X):
         heat_out[x:x + 1, :] = heat[x, 0:1, W:2 * W]
     heat_copy = send(heat_out, heat_in, device(0, 0, 1))
-
-    for copy in loads:
-        copy.wait()
-    halved = [0.5 * tile for tile in blocks(diff)]
-    sy_out[0] = edge_pack(blocks(temp) + halved, True)
-    flank_in = [send(sy_out.at[0], sy_in.at[0], ahead)]
-    sy_out[1] = edge_pack(blocks(temp) + halved, False)
-    flank_in.append(send(sy_out.at[1], sy_in.at[1], behind))
 
     lane = lanes_like((D, W))
     depth = rows_like((D, W))
@@ -322,12 +320,29 @@
 
     inner = range(1, X - 1)
     own = {x: [i for i in range(COUNT) if 0 <= x - VELOCITIES[i][0] < X] for x in range(X)}
+    def send_face(first_one, last_one):
+        for side, (edge, dx) in enumerate(ends):
+            for k in range(first_one, last_one):
+                px_out[side, k] = move(ORDER[side * FACE + k], edge)
+            part = pl.ds(first_one, last_one - first_one)
+            face_in.append(
+                send(px_out.at[side, part], px_in.at[side, part], device(dx, 0, 0))
+            )
+
+    for copy in flank_edge_in:
+        copy.wait_recv()
+    send_face(1, 3)
+    for copy in loads:
+        copy.wait()
+    halved = [0.5 * tile for tile in blocks(diff)]
+    sy_out[0] = edge_pack(blocks(temp) + halved, True)
+    flank_in = [send(sy_out.at[0], sy_in.at[0], ahead)]
+    sy_out[1] = edge_pack(blocks(temp) + halved, False)
+    flank_in.append(send(sy_out.at[1], sy_in.at[1], behind))
+
     for copy in edge_in:
         copy.wait_recv()
-    for side, (edge, dx) in enumerate(((X - 1, 1), (0, -1))):
-        for k in range(FACE):
-            px_out[side, k] = move(ORDER[side * FACE + k], edge)
-        face_in.append(send(px_out.at[side], px_in.at[side], device(dx, 0, 0)))
+    send_face(3, FACE)
     for copy in planes:
         copy.wait()
     for copy in flank_in + [heat_copy]:
@@ -389,8 +404,8 @@
         vmem(2, tall, LANES), vmem(2, tall, LANES),
         vmem(2, D, W), pair, pair,
         pltpu.SemaphoreType.DMA((X + 6,)),
-        pltpu.SemaphoreType.DMA((18,)),
-        pltpu.SemaphoreType.DMA((18,)),
+        pltpu.SemaphoreType.DMA((22,)),
+        pltpu.SemaphoreType.DMA((22,)),
     ]
     far = pl.BlockSpec(memory_space=pltpu.HBM)
     local = pl.BlockSpec(memory_space=pltpu.VMEM)

time: 17.7 us -> 17.9 us (1.011)
  Pallas kernels: 16.9 us -> 17.1 us
where the time goes in v6:
time: 17.9 us; the launch traced here: 17.7 us
  Pallas kernels  17.1 us (96%)
  between operations  0.64 us (4%)
    pallas_call x1, Pallas kernels, body(): pl.pallas_call(functools.partial(kernel, sizes), out_shape=(pltpu.VMEM(po...  16 us
    pallas_call x1, Pallas kernels, body(): pl.pallas_call(deliver, out_shape=(pltpu.HBM(populations.shape, jnp.float...  1.08 us

profile of v6, /device:TPU:0, one launch (start us, length us, event | category | flops | bytes accessed | tf_op | source)
XLA Modules:
  0.0 17.7 jit_solution(18123620979312436784)
XLA Ops:
  0.6 16.0 %shard_map.86 = (f32[19,4,16,256]{3,2,1,0:T(8,128)S(1)}, f32[4,64,128]{2,1,0:T(8,128)S(1)}) custom-call(f32[19,4,16,256]{3,2,1,0:T(8,128)} %pops_ref.1, f32[4,64,128]{2,1,0:T(8,128)} %temp_ref.1, f32[4,64,128]{2,1,0:T(8,128)} %diff_ref.1, s32[4,256]{1,0:T(4,128)} %nozzle_hbm.1, s32[4,256]{1,0:T(4,128)} %wall_hbm.1, f32[4,128]{1,0:T(4,128)} %load_hbm.1, ...), custom_call_target="tpu_custom_call" | custom-call | tf_op jit(solution)/shard_map/pallas_call | solution.py:412
  16.6 1.1 %shard_map.87 = (f32[19,4,16,256]{3,2,1,0:T(8,128)}, f32[4,64,128]{2,1,0:T(8,128)}) custom-call(f32[19,4,16,256]{3,2,1,0:T(8,128)S(1)} %get-tuple-element.4.moved_ref, f32[4,64,128]{2,1,0:T(8,128)S(1)} %get-tuple-element.5.swept_ref), custom_call_target="tpu_custom_call" | custom-call | tf_op jit(solution)/shard_map/pallas_call | solution.py:429

commit v7 on v4

--- a/solution.py
+++ b/solution.py
@@ -169,6 +169,14 @@
         sink_in.append(send(temp_ref.at[edge], sx_in.at[side, 0], device(dx, 0, 0)))
         sink_in.append(send(diff_ref.at[edge], sx_in.at[side, 1], device(dx, 0, 0)))
 
+    for copy in loads:
+        copy.wait()
+    halved = [0.5 * tile for tile in blocks(diff)]
+    sy_out[0] = edge_pack(blocks(temp) + halved, True)
+    flank_in = [send(sy_out.at[0], sy_in.at[0], ahead)]
+    sy_out[1] = edge_pack(blocks(temp) + halved, False)
+    flank_in.append(send(sy_out.at[1], sy_in.at[1], behind))
+
     def collide_plane(step, carry):
         x = lax.rem(step + X - 1, X)
         pltpu.make_async_copy(pops_ref.at[:, x], pops.at[:, x], load_sem.at[x]).wait()
@@ -184,6 +192,10 @@
 
     lax.fori_loop(0, X, collide_plane, 0)
     face_in, edge_in = [], []
+
+    for x in range(X):
+        heat_out[x:x + 1, :] = heat[x, 0:1, W:2 * W]
+    heat_copy = send(heat_out, heat_in, device(0, 0, 1))
 
     for side, (lane, dy) in enumerate(((Y - LANES, 1), (0, -1))):
         tiles = [
@@ -207,18 +219,6 @@
     edge_in.append(send(pz_out, pz_in, device(0, 0, 1)))
     for side, s in enumerate((1, -1)):
         edge_in.append(send(yz_out.at[side], yz_in.at[side], device(0, s, 1)))
-
-    for x in range(X):
-        heat_out[x:x + 1, :] = heat[x, 0:1, W:2 * W]
-    heat_copy = send(heat_out, heat_in, device(0, 0, 1))
-
-    for copy in loads:
-        copy.wait()
-    halved = [0.5 * tile for tile in blocks(diff)]
-    sy_out[0] = edge_pack(blocks(temp) + halved, True)
-    flank_in = [send(sy_out.at[0], sy_in.at[0], ahead)]
-    sy_out[1] = edge_pack(blocks(temp) + halved, False)
-    flank_in.append(send(sy_out.at[1], sy_in.at[1], behind))
 
     lane = lanes_like((D, W))
     depth = rows_like((D, W))
@@ -322,24 +322,22 @@
 
     inner = range(1, X - 1)
     own = {x: [i for i in range(COUNT) if 0 <= x - VELOCITIES[i][0] < X] for x in range(X)}
+    for copy in planes:
+        copy.wait()
+    for copy in flank_in + [heat_copy] + sink_in:
+        copy.wait_recv()
+    first_in = []
+    for side, (edge, dx) in enumerate(((X - 1, 1), (0, -1))):
+        sweep_first(edge)
+        first_in.append(send(first.at[edge], fx_in.at[side], device(dx, 0, 0)))
     for copy in edge_in:
         copy.wait_recv()
     for side, (edge, dx) in enumerate(((X - 1, 1), (0, -1))):
         for k in range(FACE):
             px_out[side, k] = move(ORDER[side * FACE + k], edge)
         face_in.append(send(px_out.at[side], px_in.at[side], device(dx, 0, 0)))
-    for copy in planes:
-        copy.wait()
-    for copy in flank_in + [heat_copy]:
-        copy.wait_recv()
     for x in inner:
         sweep_first(x)
-    for copy in sink_in:
-        copy.wait_recv()
-    first_in = []
-    for side, (edge, dx) in enumerate(((X - 1, 1), (0, -1))):
-        sweep_first(edge)
-        first_in.append(send(first.at[edge], fx_in.at[side], device(dx, 0, 0)))
     fy_out[0] = edge_pack(blocks(first), True)
     beside_in = [send(fy_out.at[0], fy_in.at[0], ahead)]
     fy_out[1] = edge_pack(blocks(first), False)

time: 17.7 us -> 18.5 us (1.045)
  Pallas kernels: 16.9 us -> 17.7 us
    pallas_call x1, Pallas kernels: 15.9 us -> 16.6 us  [body(): pl.pallas_call(functools.partial(kernel, sizes), out_shape=(pltpu.VMEM(po...]
where the time goes in v7:
time: 18.5 us; the launch traced here: 18.3 us
  Pallas kernels  17.7 us (96%)
  between operations  0.64 us (3%)
    pallas_call x1, Pallas kernels, body(): pl.pallas_call(functools.partial(kernel, sizes), out_shape=(pltpu.VMEM(po...  16.6 us
    pallas_call x1, Pallas kernels, body(): pl.pallas_call(deliver, out_shape=(pltpu.HBM(populations.shape, jnp.float...  1.08 us

profile of v7, /device:TPU:0, one launch (start us, length us, event | category | flops | bytes accessed | tf_op | source)
XLA Modules:
  0.0 18.3 jit_solution(17074827239784785998)
XLA Ops:
  0.6 16.6 %shard_map.86 = (f32[19,4,16,256]{3,2,1,0:T(8,128)S(1)}, f32[4,64,128]{2,1,0:T(8,128)S(1)}) custom-call(f32[19,4,16,256]{3,2,1,0:T(8,128)} %pops_ref.1, f32[4,64,128]{2,1,0:T(8,128)} %temp_ref.1, f32[4,64,128]{2,1,0:T(8,128)} %diff_ref.1, s32[4,256]{1,0:T(4,128)} %nozzle_hbm.1, s32[4,256]{1,0:T(4,128)} %wall_hbm.1, f32[4,128]{1,0:T(4,128)} %load_hbm.1, ...), custom_call_target="tpu_custom_call" | custom-call | tf_op jit(solution)/shard_map/pallas_call | solution.py:395
  17.2 1.1 %shard_map.87 = (f32[19,4,16,256]{3,2,1,0:T(8,128)}, f32[4,64,128]{2,1,0:T(8,128)}) custom-call(f32[19,4,16,256]{3,2,1,0:T(8,128)S(1)} %get-tuple-element.4.moved_ref, f32[4,64,128]{2,1,0:T(8,128)S(1)} %get-tuple-element.5.swept_ref), custom_call_target="tpu_custom_call" | custom-call | tf_op jit(solution)/shard_map/pallas_call | solution.py:412
